TPU v7x, 128 devices: a whole 4x4x4 slice. The times are simulated.
128 devices in a mesh: dp: 16 (over z, x_lo, core), row: 4 (over y), col: 2 (over x_hi).
Axes of the slice: x: 4 (x_hi: 2, x_lo: 2; x = x_hi * 2 + x_lo), y: 4, z: 4, core: 2. Of those that a mesh axis runs over, the one named last changes fastest.
Arguments:
- tokens: bfloat16 [16384, 1536], P(('dp', 'col'), 'row'), may hold values from -6 to 6
- cotangent: bfloat16 [16384, 1536], P(('dp', 'col'), 'row'), may hold values from -6 to 6
- lengths: int32 [16, 3], P('dp'), may hold values from 1 to 896, 1024 in all within a row
- gain_attn: float32 [1536], P('row'), may hold values from 0.5 to 1.5
- w_query: bfloat16 [1536, 1536], P('row', 'col'), may hold values from -0.15625 to 0.15625
- key_projection: bfloat16 [1536, 256], P('row', 'col'), may hold values from -0.15625 to 0.15625
- value_projection: bfloat16 [1536, 256], P('row', 'col'), may hold values from -0.15625 to 0.15625
- bias_query: float32 [1536], P('col'), may hold values from -3 to 3
- key_bias_vector: float32 [256], P('col'), may hold values from -3 to 3
- value_bias_vector: float32 [256], P('col'), may hold values from -3 to 3
- w_out: bfloat16 [1536, 1536], P('col', 'row'), may hold values from -1.25 to 1.25
- gain_ffn: float32 [1536], P('row'), may hold values from 0.5 to 1.5
- w_gate: bfloat16 [1536, 8960], P('row', 'col'), may hold values from -0.15625 to 0.15625
- w_up: bfloat16 [1536, 8960], P('row', 'col'), may hold values from -0.15625 to 0.15625
- w_down: bfloat16 [8960, 1536], P('col', 'row'), may hold values from -0.0625 to 0.0625
Outputs:
- result: float32 [16384, 1536], P(('dp', 'col'), 'row')
- grad_tokens: float32 [16384, 1536], P(('dp', 'col'), 'row')
- grad_gain_attn: float32 [1536], P('row')
- grad_w_query: float32 [1536, 1536], P('row', 'col')
- grad_w_key: float32 [1536, 256], P('row', 'col')
- grad_w_value: float32 [1536, 256], P('row', 'col')
- grad_bias_query: float32 [1536], P('col')
- grad_bias_key: float32 [256], P('col')
- grad_bias_value: float32 [256], P('col')
- grad_w_out: float32 [1536, 1536], P('col', 'row')
- grad_gain_ffn: float32 [1536], P('row')
- grad_w_gate: float32 [1536, 8960], P('row', 'col')
- grad_w_up: float32 [1536, 8960], P('row', 'col')
- grad_w_down: float32 [8960, 1536], P('col', 'row')
Inputs may be any that keep to these rules, and one draw needn't show every extreme that they name: In each group the 3 lengths sum to 1024 and the longest is 896.
All inputs are finite; a program needn't handle non-finite values.
Results may differ from a plain program's by a relative error of at most 0.04.
Values may be sent and summed in bfloat16 or wider, within the bound.
A program may use at most 192 MiB of HBM per device.

v0:
```python
import math

import jax
import jax.numpy as jnp
from jax import lax
from jax.experimental import pallas as pl
from jax.experimental.pallas import tpu as pltpu
from jax.sharding import PartitionSpec as P

HEAD_SIZE = 128
EPS = 1e-06
THETA = 1000000.0
LANES = 128
MESH = pl.DeviceIdType.MESH
BF16 = jnp.bfloat16
F32 = jnp.float32
ANY = pl.BlockSpec(memory_space=pl.ANY)
VMEM = pl.BlockSpec(memory_space=pltpu.VMEM)

Z_STEP = 4
FRONT_COPIES = 77
FRONT_LOCAL = 27
BACK_COPIES = 119
BACK_LOCAL = 26


def here():
    return lax.axis_index("dp"), lax.axis_index("row"), lax.axis_index("col")


def flip_near(dp):
    return dp + 2 - 4 * ((dp // 2) % 2)


def pair_of(place, row=None):
    dp, own, col = place
    return flip_near(dp), own if row is None else row, 1 - col


def near_of(place, row=None):
    dp, own, col = place
    return flip_near(dp), own if row is None else row, col


def twin_of(place):
    dp, row, col = place
    return dp + 1 - 2 * (dp % 2), row, col


def along_z(place, step):
    dp, row, col = place
    return (dp + Z_STEP * step) % (4 * Z_STEP), row, col


def along_y(place, step):
    dp, row, col = place
    return dp, (row + step) % 4, col


def meet(peers):
    barrier = pltpu.get_barrier_semaphore()
    for peer in peers:
        pl.semaphore_signal(barrier, inc=1, device_id=peer, device_id_type=MESH)
    pl.semaphore_wait(barrier, len(peers))


class Mail:
    def __init__(self, send, recv):
        self.send, self.recv, self.count, self.sent = send, recv, 0, []

    def post(self, source, target, device):
        index = self.count
        self.count += 1
        copy = pltpu.make_async_remote_copy(
            src_ref=source,
            dst_ref=target,
            send_sem=self.send.at[index],
            recv_sem=self.recv.at[index],
            device_id=device,
            device_id_type=MESH,
        )
        copy.start()
        self.sent.append(copy)
        return copy

    def finish(self):
        assert self.count == self.send.shape[0], (self.count, self.send.shape)
        for copy in self.sent:
            copy.wait_send()


def talk(body, ident, copies, local, outs, in_specs, out_specs, scratch=(), limit=32):
    return pl.pallas_call(
        body,
        out_shape=[jax.ShapeDtypeStruct(*out) for out in outs],
        in_specs=in_specs,
        out_specs=out_specs,
        scratch_shapes=[
            *scratch,
            pltpu.SemaphoreType.DMA((copies,)),
            pltpu.SemaphoreType.DMA((copies,)),
            pltpu.SemaphoreType.DMA((max(local, 1),)),
        ],
        compiler_params=pltpu.CompilerParams(
            collective_id=ident, has_side_effects=True, vmem_limit_bytes=limit << 20
        ),
    )


def front_kernel(
    tok,
    cot,
    lens_in,
    gain_attn,
    gain_ffn,
    bias_q,
    bias_k,
    bias_v,
    wq,
    wk,
    wv,
    wo,
    wg,
    wu,
    wd,
    tok_out,
    cot_full,
    gains_out,
    normed,
    query,
    kva_out,
    kvb_out,
    logs,
    attended,
    tables,
    middle,
    turned_a,
    turned_b,
    normed_ffn,
    w_in_out,
    w_out_out,
    wgu_full,
    wd_full,
    lens,
    gains,
    tok_v,
    lens_v,
    gains_v,
    w_in,
    w_out,
    gu_own,
    wd_own,
    blank_gu,
    blank_wd,
    kv,
    kva,
    kvb,
    bias_a,
    bias_b,
    branch,
    branch_in,
    send,
    recv,
    local,
):
    place = here()
    dp, row, col = place
    z, core = dp // Z_STEP, dp % 2
    twin, pair, up, down = twin_of(place), pair_of(place), along_z(place, 1), along_z(place, 3)
    right, left, near = along_y(place, 1), along_y(place, 3), near_of(place)
    meet(
        [along_y(place, s) for s in (1, 2, 3)]
        + [near_of(place, (row + s) % 4) for s in range(4)]
        + [pair, twin, up, down]
    )
    mail = Mail(send, recv)
    kept = []

    def keep(source, target):
        kept.append(pltpu.make_async_copy(source, target, local.at[len(kept)]))
        kept[-1].start()
        return len(kept) - 1

    def kept_wait(index):
        kept[index].wait()
        kept[index] = None

    def even(start, size):
        return pl.ds(pl.multiple_of(start, 16), size)

    rows, piece = tok.shape[0] // 4, tok.shape[1]
    width = 4 * piece
    own_rows = even(col * rows, rows)
    spot = even(row * rows, rows)

    def spread(source, target):
        got = []
        for step in range(4):
            part = source.at[even(((row + step) % 4) * rows, rows), :]
            lanes = pl.ds(((4 - step) % 4) * piece, piece)
            if step:
                got.append(mail.post(part, target.at[own_rows, lanes], along_y(place, step)))
            else:
                mine = keep(part, target.at[own_rows, lanes])
        return got, mine

    tokens = spread(tok, tok_v)
    lens[...] = jnp.zeros_like(lens)
    lens[0:1, 0 : lens_in.shape[1]] = lens_in[...]
    gains[...] = jnp.zeros_like(gains)
    gains[0:1, :] = gain_attn[...].reshape(1, piece)
    gains[1:2, :] = gain_ffn[...].reshape(1, piece)
    lens_got = mail.post(lens, lens_v.at[col], pair)
    lens_kept = keep(lens, lens_v.at[col])
    gains_kept = keep(gains, gains_v.at[0])
    gains_got = [mail.post(gains, gains_v.at[4 - s], along_y(place, s)) for s in (1, 2, 3)]

    q_width, kv_width = wq.shape[1], wk.shape[1]
    stages = [
        keep(wq, w_in.at[0, :, pl.ds(0, q_width)]),
        keep(wk, w_in.at[0, :, pl.ds(q_width, kv_width)]),
        keep(wv, w_in.at[0, :, pl.ds(q_width + kv_width, kv_width)]),
        keep(wo, w_out.at[:, pl.ds(0, piece)]),
    ]
    share = wd_own.shape[0]
    thin = piece // 2
    sure = share - LANES
    take = pl.multiple_of(z * share, LANES)
    big = []
    for k in range(2):
        for i, source in enumerate((wg, wu)):
            from_rows = pl.ds(k * thin, thin)
            big.append(keep(source.at[from_rows, pl.ds(take, sure)], gu_own.at[k, :, pl.ds(i * share, sure)]))
    big.append(keep(wd.at[pl.ds(take, sure), :], wd_own.at[pl.ds(0, sure), :]))
    blank_gu[...] = jnp.zeros_like(blank_gu)
    blank_wd[...] = jnp.zeros_like(blank_wd)
    first_edge = len(kept)
    edges = []
    for k in range(2):
        for i, source in enumerate((wg, wu)):
            target = gu_own.at[k, :, pl.ds(i * share + sure, LANES)]
            edges.append((source, pl.ds(k * thin, thin), None, target, blank_gu))
    edges.append((wd, None, slice(None), wd_own.at[pl.ds(sure, LANES), :], blank_wd))

    def edge(index, last):
        source, from_rows, _, target, blank = edges[index]
        if last:
            origin = blank
        elif from_rows is None:
            origin = source.at[pl.ds(pl.multiple_of(take + sure, LANES), LANES), :]
        else:
            origin = source.at[from_rows, pl.ds(pl.multiple_of(take + sure, LANES), LANES)]
        return pltpu.make_async_copy(origin, target, local.at[first_edge + index])

    @pl.when(z < 3)
    def _():
        for index in range(len(edges)):
            edge(index, False).start()

    @pl.when(z == 3)
    def _():
        for index in range(len(edges)):
            edge(index, True).start()

    for index in range(len(edges)):
        kept.append(edge(index, True))
        big.append(first_edge + index)

    q_rows, o_rows = thin // 4, w_out.shape[0] // 8

    def in_part(j, owner_z):
        return w_in.at[j, even(core * thin + owner_z * q_rows, q_rows), :]

    def in_parts(owner_z):
        return w_in.at[pl.ds(1, 3), even(core * thin + owner_z * q_rows, q_rows), :]

    def in_side(owner_z, side):
        lanes = pl.ds(side * (w_in.shape[2] // 2), w_in.shape[2] // 2)
        return w_in.at[pl.ds(1, 3), even(core * thin + owner_z * q_rows, q_rows), lanes]

    def out_part(j, owner_z):
        return w_out.at[even(core * 4 * o_rows + owner_z * o_rows, o_rows), pl.ds(j * piece, piece)]

    def out_parts(owner_z):
        return w_out.at[even(core * 4 * o_rows + owner_z * o_rows, o_rows), pl.ds(piece, 3 * piece)]

    def out_side(owner_z, side):
        start = core * 4 * o_rows + owner_z * o_rows + side * (o_rows // 2)
        return w_out.at[even(start, o_rows // 2), pl.ds(piece, 3 * piece)]

    for index in stages:
        kept_wait(index)
    in_got = [mail.post(in_part(0, z), in_part(4 - step, z), along_y(place, step)) for step in (1, 3, 2)]

    def to_pair(spreading, target):
        got, mine = spreading
        kept_wait(mine)
        for copy in got:
            copy.wait_recv()
        return mail.post(target.at[own_rows, :], target.at[own_rows, :], pair)

    tokens_pair = to_pair(tokens, tok_v)
    shares = []

    def give(part):
        shares.append(mail.post(part, part, twin))

    def z_first(side):
        copies = {}
        for turn in range(2):
            copies["u", turn] = mail.post(side(z, turn), side(z, turn), up)
            copies["d", 1 - turn] = mail.post(side(z, 1 - turn), side(z, 1 - turn), down)
        return copies

    below, above, across = (z + 3) % 4, (z + 1) % 4, (z + 2) % 4

    def z_second(side, whole, copies):
        copies["u", 0].wait_recv()
        far_up = mail.post(side(below, 0), side(below, 0), up)
        copies["d", 1].wait_recv()
        far_down = mail.post(side(above, 1), side(above, 1), down)
        copies["u", 1].wait_recv()
        give(whole(below))
        copies["d", 0].wait_recv()
        give(whole(above))
        return far_up, far_down

    def z_third(whole, copies):
        for copy in copies:
            copy.wait_recv()
        give(whole(across))

    for copy in in_got:
        copy.wait_recv()
    in_z = z_first(in_side)
    give(in_parts(z))
    out_got = [mail.post(out_part(0, z), out_part(4 - step, z), along_y(place, step)) for step in (1, 3, 2)]
    cotangents = spread(cot, cot_full.at[0])
    for index in big:
        kept_wait(index)
    x_lo = (dp // 2) % 2
    gu_half, wd_half = thin // 4, share // 4

    def gu_part(j, which=None, owner=x_lo):
        start, size = (0, 2 * gu_half) if which is None else (which * gu_half, gu_half)
        return wgu_full.at[j, core, even(owner * 2 * gu_half + start, size), :]

    def gu_whole(j):
        return wgu_full.at[j, core]

    def wd_part(j, which=None):
        start, size = (0, 2 * wd_half) if which is None else (which * wd_half, wd_half)
        return wd_full.at[even(core * 2 * wd_half + start, size), pl.ds(j * piece, piece)]

    def gu_source(which):
        return gu_own.at[core, even((x_lo * 2 + which) * gu_half, gu_half), :]

    def wd_source(which):
        return wd_own.at[even((core * 2 + which) * wd_half, wd_half), :]

    y_ring, near_gu, twins = {}, [], []

    def y_start(name, source, part):
        for turn in range(2):
            y_ring[name, "r", turn] = mail.post(source(turn), part(3, turn), right)
            y_ring[name, "l", 1 - turn] = mail.post(source(1 - turn), part(1, 1 - turn), left)

    def y_forward(name, part):
        y_ring[name, "r", 0].wait_recv()
        y_ring[name, "fr"] = mail.post(part(3, 0), part(2, 0), right)
        y_ring[name, "l", 1].wait_recv()
        y_ring[name, "fl"] = mail.post(part(1, 1), part(2, 1), left)

    def y_share(name, part, queue, device):
        y_ring[name, "r", 1].wait_recv()
        queue.append(mail.post(part(3), part(3), device))
        y_ring[name, "l", 0].wait_recv()
        queue.append(mail.post(part(1), part(1), device))

    def y_end(name, part, queue, device):
        y_ring[name, "fr"].wait_recv()
        y_ring[name, "fl"].wait_recv()
        queue.append(mail.post(part(2), part(2), device))


    kept_wait(lens_kept)
    lens_got.wait_recv()
    half_rows = 4 * rows

    def segment_of(which, index):
        end_0 = lens_v[which, 0:1, 0:1]
        end_1 = end_0 + lens_v[which, 0:1, 1:2]
        past_0 = (index >= end_0).astype(jnp.int32)
        past_1 = (index >= end_1).astype(jnp.int32)
        start = jnp.where(past_1 > 0, end_1, jnp.where(past_0 > 0, end_0, 0))
        return past_0 + past_1, start

    lane = lax.broadcasted_iota(jnp.int32, (rows, HEAD_SIZE), 1)
    half_lane = jnp.where(lane >= HEAD_SIZE // 2, lane - HEAD_SIZE // 2, lane).astype(F32)
    inverse = jnp.exp(half_lane * (-2.0 * math.log(THETA) / HEAD_SIZE))
    for which, mask, mask_t, key_count in ((0, bias_a, turned_a, half_rows), (1, bias_b, turned_b, 2 * half_rows)):
        index = lax.broadcasted_iota(jnp.int32, (rows, HEAD_SIZE), 0) + (row * rows + which * half_rows)
        _, start = segment_of(which, index)
        turn = (index - start).astype(F32) * inverse
        tables[0, which * rows : (which + 1) * rows, :] = jnp.cos(turn)
        sine = jnp.sin(turn)
        tables[1, which * rows : (which + 1) * rows, :] = jnp.where(lane >= HEAD_SIZE // 2, sine, -sine)
        at = lax.broadcasted_iota(jnp.int32, (rows, key_count), 0) + (row * rows + which * half_rows)
        keys = lax.broadcasted_iota(jnp.int32, (rows, key_count), 1)
        allowed = jnp.logical_and(segment_of(which, at)[0] == segment_of(which, keys)[0], keys <= at)
        mask[...] = jnp.where(allowed, 0.0, -1e30)
        at = lax.broadcasted_iota(jnp.int32, (key_count, rows), 1) + (row * rows + which * half_rows)
        keys = lax.broadcasted_iota(jnp.int32, (key_count, rows), 0)
        allowed = jnp.logical_and(segment_of(which, at)[0] == segment_of(which, keys)[0], keys <= at)
        mask_t[...] = jnp.where(allowed, 0.0, -1e30)

    kept_wait(gains_kept)
    for copy in gains_got:
        copy.wait_recv()
    keep(gains_v, gains_out)

    def normalise(value, which):
        scale = lax.rsqrt(jnp.sum(value * value, -1, keepdims=True) * (1.0 / width) + EPS)
        return [
            (value[:, j * piece : (j + 1) * piece] * scale * gains_v[j, which : which + 1, :]).astype(BF16)
            for j in range(4)
        ]

    def norm_rows(which):
        part = pl.ds(pl.multiple_of(which * rows, rows), rows)
        for j, block in enumerate(normalise(tok_v[part, :].astype(F32), 0)):
            normed[part, pl.ds(j * piece, piece)] = block

    norm_rows(col)
    for copy in out_got:
        copy.wait_recv()
    give(out_parts(z))
    y_start("gu", gu_source, gu_part)
    keep(gu_own, wgu_full.at[0])
    keep(wd_own, wd_full.at[:, pl.ds(0, piece)])
    in_far = z_second(in_side, in_parts, in_z)
    out_z = z_first(out_side)
    tokens_pair.wait_recv()
    keep(tok_v, tok_out)
    norm_rows(1 - col)
    cot_pair = to_pair(cotangents, cot_full.at[0])
    z_third(in_parts, in_far)
    for copy in shares:
        copy.wait_recv()
    shares.clear()
    keep(w_in, w_in_out)

    in_width = w_in.shape[2]

    def project(lanes, bias):
        weights = w_in[:, :, lanes]
        weights = weights.reshape(4 * weights.shape[1], weights.shape[2])
        return jnp.dot(normed[...], weights, preferred_element_type=F32) + bias

    def rotate(value):
        return value * tables[0] + pltpu.roll(value, HEAD_SIZE // 2, 1) * tables[1]

    key_value = project(slice(q_width, in_width), jnp.concatenate([bias_k[...].reshape(1, kv_width), bias_v[...].reshape(1, kv_width)], 1))
    kv[:, 0:kv_width] = rotate(key_value[:, 0:kv_width]).astype(BF16)
    kv[:, kv_width : 2 * kv_width] = key_value[:, kv_width : 2 * kv_width].astype(BF16)
    a_rows, b_rows = pl.ds(0, rows), pl.ds(rows, rows)
    high_spot = even(half_rows + row * rows, rows)
    a_got, b_got = [], []
    for step in (1, 2, 3):
        a_got.append(mail.post(kv.at[a_rows, :], kva.at[spot, :], along_y(place, step)))
    for step in range(4):
        b_got.append(mail.post(kv.at[a_rows, :], kvb.at[spot, :], near_of(place, (row + step) % 4)))
        if step:
            b_got.append(mail.post(kv.at[b_rows, :], kvb.at[high_spot, :], along_y(place, step)))
    kva[spot, :] = kv[a_rows, :]
    kvb[high_spot, :] = kv[b_rows, :]
    for first in range(0, q_width, 2 * HEAD_SIZE):
        value = project(slice(first, first + 2 * HEAD_SIZE), bias_q[first : first + 2 * HEAD_SIZE].reshape(1, 2 * HEAD_SIZE))
        for i in range(2):
            lanes = slice(first + i * HEAD_SIZE, first + (i + 1) * HEAD_SIZE)
            query[:, lanes] = rotate(value[:, i * HEAD_SIZE : (i + 1) * HEAD_SIZE]).astype(BF16)

    y_forward("gu", gu_part)
    y_share("gu", gu_part, near_gu, near)
    out_far = z_second(out_side, out_parts, out_z)
    heads = q_width // HEAD_SIZE
    factor = HEAD_SIZE ** (-0.5)

    def attend(half, keys, mask):
        part = slice(half * rows, (half + 1) * rows)

        @pl.loop(0, heads)
        def _(h):
            lanes = pl.ds(pl.multiple_of(h * HEAD_SIZE, LANES), HEAD_SIZE)
            raw = lax.dot_general(
                query[part, lanes], keys[:, 0:HEAD_SIZE], (((1,), (1,)), ((), ())), preferred_element_type=F32
            )
            scores = raw * factor + mask[...]
            peak = jnp.max(scores, -1, keepdims=True)
            raised = jnp.exp(scores - peak)
            total = jnp.sum(raised, -1, keepdims=True)
            probs = (raised * (1.0 / total)).astype(BF16)
            out = jnp.dot(probs, keys[:, HEAD_SIZE : 2 * HEAD_SIZE], preferred_element_type=F32)
            attended[part, lanes] = out.astype(BF16)
            logs[half * heads + h] = jnp.broadcast_to(peak + jnp.log(total), (rows, LANES)).T[0:8, :]

        for first in range(0, width, piece):
            lanes = slice(first, first + piece)
            branch[part, lanes] = jnp.dot(
                attended[part, :], w_out[:, lanes], preferred_element_type=F32
            ).astype(BF16)
        return mail.post(branch.at[part, :], branch_in.at[part, :], pair)

    def finish_half(half, copy):
        part = slice(half * rows, (half + 1) * rows)
        copy.wait_recv()
        value = tok_v[part, :].astype(F32) + (branch[part, :].astype(F32) + branch_in[part, :].astype(F32))
        middle[part, :] = value
        for j, block in enumerate(normalise(value, 1)):
            normed_ffn[part, j * piece : (j + 1) * piece] = block

    def z_send(source, target, half):
        part = pl.ds(half * rows, rows)
        return (
            mail.post(source.at[part, :], target.at[1, part, :], up),
            mail.post(source.at[part, :], target.at[3, part, :], down),
        )

    def z_forward(target, half, copies):
        part = pl.ds(half * rows, rows)
        if half == 0:
            copies[0].wait_recv()
            return copies[1], mail.post(target.at[1, part, :], target.at[2, part, :], up)
        copies[1].wait_recv()
        return copies[0], mail.post(target.at[3, part, :], target.at[2, part, :], down)

    cot_pair.wait_recv()
    cot_z = [z_send(cot_full.at[0], cot_full, half) for half in range(2)]
    for copy in a_got:
        copy.wait_recv()
    keep(kva, kva_out)
    z_third(out_parts, out_far)
    for copy in shares:
        copy.wait_recv()
    keep(w_out, w_out_out)
    swap_a = attend(0, kva, bias_a)
    for copy in b_got:
        copy.wait_recv()
    keep(kvb, kvb_out)
    y_start("wd", wd_source, wd_part)
    swap_b = attend(1, kvb, bias_b)
    y_end("gu", gu_part, near_gu, near)
    finish_half(0, swap_a)
    y_forward("wd", wd_part)
    cot_last = [z_forward(cot_full, half, cot_z[half]) for half in range(2)]
    y_share("wd", wd_part, twins, twin)
    finish_half(1, swap_b)
    for j, copy in zip((3, 1, 2), near_gu):
        copy.wait_recv()
        twins.append(mail.post(gu_whole(j), gu_whole(j), twin))
    y_end("wd", wd_part, twins, twin)
    for copies in cot_last:
        for copy in copies:
            copy.wait_recv()
    for copy in twins:
        copy.wait_recv()
    for copy in kept:
        if copy is not None:
            copy.wait()
    mail.finish()


def ffn_kernel(
    normed,
    cot,
    wgu,
    wd,
    total,
    gu_sum,
    dn_half,
    result_sum,
    x,
    cot_v,
    wgu_v,
    wd_v,
    gb,
    act,
    parts,
    turned,
    down_v,
    gu_in,
    dn_in,
    up1,
    down1,
    up2,
    down2,
    other,
    stage_up,
    stage_down,
    stage,
    res_up1,
    res_down1,
    res_up2,
    res_down2,
    gu_up1,
    gu_down1,
    gu_up2,
    gu_down2,
    send,
    recv,
    local,
):
    place = here()
    dp, row, col = place
    core = dp % 2
    up, down, pair, twin = along_z(place, 1), along_z(place, 3), pair_of(place), twin_of(place)
    right, left = along_y(place, 1), along_y(place, 3)
    meet([up, down, pair, twin, right, left])
    mail = Mail(send, recv)
    order = ((0, 0), (0, 1), (1, 0), (3, 1), (2, 0), (2, 1), (1, 1), (3, 0))
    spots = {half: i for i, half in enumerate(order)}
    rows = normed.shape[0] // 2
    size = rows // 2

    def block(ref, slot, half):
        return ref.at[pl.ds(spots[slot, half] * rows, rows), :]

    def halves(ref, half):
        return ref.at[pl.ds(half * rows, rows), :]

    kept = []

    def keep(source, target):
        kept.append(pltpu.make_async_copy(source, target, local.at[len(kept)]))
        kept[-1].start()
        return len(kept) - 1

    def kept_wait(index):
        kept[index].wait()
        kept[index] = None

    got = {}

    def z_start(which):
        got["u", which] = mail.post(halves(normed, which), block(x, 1, which), up)
        got["d", 1 - which] = mail.post(halves(normed, 1 - which), block(x, 3, 1 - which), down)

    z_start(0)
    share = wd.shape[0]
    early = [keep(normed, x.at[pl.ds(0, 2 * rows), :]), keep(wgu, wgu_v)]
    early.append(keep(cot.at[0], cot_v.at[pl.ds(0, 2 * rows), :]))
    early.append(keep(wd, wd_v))
    later = [keep(cot.at[slot, pl.ds(half * rows, rows), :], block(cot_v, slot, half)) for slot, half in order[2:]]
    width = normed.shape[1]
    piece = width // 4

    def dot_nt(left, right):
        return lax.dot_general(left, right, (((1,), (1,)), ((), ())), preferred_element_type=F32)

    def compute(c):
        part = slice(2 * rows * c, 2 * rows * (c + 1))
        for start, size in ((0, 512), (512, share - 512)):
            lanes, above = slice(start, start + size), slice(share + start, share + start + size)
            gate = jnp.dot(x[part, :], wgu_v[:, lanes], preferred_element_type=F32)
            value = jnp.dot(x[part, :], wgu_v[:, above], preferred_element_type=F32)
            grad = dot_nt(cot_v[part, :], wd_v[lanes, :])
            spread = 1.0 / (1.0 + jnp.exp(-gate))
            smooth = gate * spread
            act[part, lanes] = (smooth * value).astype(BF16)
            gb[part, lanes] = (grad * value * (spread * (1.0 + gate * (1.0 - spread)))).astype(BF16)
            gb[part, above] = (grad * smooth).astype(BF16)
        for m in range(3):
            lanes = slice(512 * m, 512 * (m + 1))
            parts[part, lanes] = dot_nt(gb[part, :], wgu_v[lanes, :]).astype(BF16)

    for index in early:
        kept_wait(index)
    compute(0)
    got["u", 0].wait_recv()
    far_up = mail.post(block(x, 1, 0), block(x, 2, 0), up)
    got["d", 1].wait_recv()
    far_down = mail.post(block(x, 3, 1), block(x, 2, 1), down)
    for index in later:
        kept_wait(index)
    compute(1)
    z_start(1)
    far_up.wait_recv()
    far_down.wait_recv()
    compute(2)
    first = {}
    for i in range(2):
        rows_i = pl.ds(i * size, size)
        first["u", i] = mail.post(block(parts, 2, 0).at[rows_i, :], up1.at[i], up)
        first["d", i] = mail.post(block(parts, 2, 1).at[rows_i, :], down1.at[i], down)
    got["u", 1].wait_recv()
    got["d", 0].wait_recv()
    compute(3)
    second = {
        ("d", 0): mail.post(block(parts, 1, 0), down2.at[0], down),
        ("u", 1): mail.post(block(parts, 3, 1), up2.at[1], up),
    }

    def turn_over(source, target):
        @pl.loop(0, source.shape[1] // LANES)
        def _(t):
            lanes = pl.ds(pl.multiple_of(t * LANES, LANES), LANES)
            target[lanes, :] = source[:, lanes].T

    def forward(i):
        rows_i = pl.ds(i * size, size)
        first["u", i].wait_recv()
        stage_up[i] = (block(parts, 3, 0).at[rows_i, :][...].astype(F32) + up1[i].astype(F32)).astype(BF16)
        second["u", 0, i] = mail.post(stage_up.at[i], up2.at[0, rows_i, :], up)
        first["d", i].wait_recv()
        stage_down[i] = (block(parts, 1, 1).at[rows_i, :][...].astype(F32) + down1[i].astype(F32)).astype(BF16)
        second["d", 1, i] = mail.post(stage_down.at[i], down2.at[1, rows_i, :], down)

    turn_over(x, turned)
    tile = 256
    tiles = 2 * share // tile

    def gu_tiles(first_tile, last_tile):
        @pl.loop(first_tile, last_tile)
        def _(n):
            lanes = pl.ds(pl.multiple_of(((n + (tiles // 2) * (1 - core)) % tiles) * tile, tile), tile)
            wgu_v[:, lanes] = jnp.dot(turned[...], gb[:, lanes], preferred_element_type=F32).astype(BF16)

    swaps = {}

    def settle(i):
        rows_i = pl.ds(i * size, size)
        if i == 0:
            second["d", 0].wait_recv()
            second["u", 1].wait_recv()
        second["u", 0, i].wait_recv()
        second["d", 1, i].wait_recv()
        for half in range(2):
            value = block(parts, 0, half).at[rows_i, :][...].astype(F32)
            value = value + up2[half, rows_i, :].astype(F32) + down2[half, rows_i, :].astype(F32)
            stage[half, rows_i, :] = value.astype(BF16)
            swaps[half, i] = mail.post(stage.at[half, rows_i, :], other.at[half, rows_i, :], pair)

    there = pl.ds(pl.multiple_of((1 - core) * share, LANES), share)
    mine = pl.ds(pl.multiple_of(core * share, LANES), share)
    gu_tiles(0, tiles // 2 + 1)
    shared = [
        mail.post(wgu_v.at[pl.ds(j * piece, piece), there], gu_in.at[j], twin) for j in range(4)
    ]
    forward(0)
    forward(1)
    gu_tiles(tiles // 2 + 1, tiles)
    for j in range(4):
        shared[j].wait_recv()
        gu_in[j] = (wgu_v[pl.ds(j * piece, piece), mine].astype(F32) + gu_in[j].astype(F32)).astype(BF16)

    def ring_y(i):
        height = piece // 3
        half = height // 2
        low, high = pl.ds(i * height, half), pl.ds(i * height + half, half)
        one, two, three, four = gu_up1.at[i], gu_down1.at[i], gu_up2.at[i], gu_down2.at[i]
        begin = (mail.post(gu_in.at[2, low, :], one, right), mail.post(gu_in.at[2, high, :], two, left))
        straight = [
            mail.post(gu_in.at[1, high, :], three.at[pl.ds(half, half), :], right),
            mail.post(gu_in.at[3, low, :], four.at[pl.ds(0, half), :], left),
        ]
        yield
        begin[0].wait_recv()
        one[...] = (gu_in[1, low, :].astype(F32) + one[...].astype(F32)).astype(BF16)
        straight.append(mail.post(one, three.at[pl.ds(0, half), :], right))
        begin[1].wait_recv()
        two[...] = (gu_in[3, high, :].astype(F32) + two[...].astype(F32)).astype(BF16)
        straight.append(mail.post(two, four.at[pl.ds(half, half), :], left))
        yield
        for copy in straight:
            copy.wait_recv()
        part = pl.ds(i * height, height)
        value = gu_in[0, part, :].astype(F32) + three[...].astype(F32) + four[...].astype(F32)
        gu_sum[part, :] = value.astype(BF16)
        yield

    rings = [ring_y(i) for i in range(3)]
    for ring in rings:
        next(ring)
    for m in range(3):
        lanes = slice(512 * m, 512 * (m + 1))

        @pl.loop(0, 4)
        def _(c):
            part = pl.ds(pl.multiple_of(c * 2 * rows, 2 * rows), 2 * rows)
            down_v[part, lanes] = jnp.dot(act[part, :], wd_v[:, lanes], preferred_element_type=F32).astype(BF16)

    result = {
        "u1": mail.post(block(down_v, 2, 0), res_up1, up),
        "d1": mail.post(block(down_v, 2, 1), res_down1, down),
        "u2": mail.post(block(down_v, 3, 1), res_up2.at[1], up),
        "d2": mail.post(block(down_v, 1, 0), res_down2.at[0], down),
    }
    settle(0)
    settle(1)
    turn_over(act, turned)

    @pl.loop(0, width // tile)
    def _(n):
        lanes = pl.ds(pl.multiple_of(n * tile, tile), tile)
        wd_v[:, lanes] = jnp.dot(
            turned[0:share, :], cot_v[:, lanes], preferred_element_type=F32
        ).astype(BF16)

    half_share = share // 2
    rows_there = pl.ds(pl.multiple_of((1 - core) * half_share, 16), half_share)
    rows_mine = pl.ds(pl.multiple_of(core * half_share, 16), half_share)
    shared += [
        mail.post(wd_v.at[rows_there, pl.ds(j * piece, piece)], dn_in.at[j], twin) for j in range(4)
    ]
    for ring in rings:
        next(ring)
    for j in range(4):
        shared[4 + j].wait_recv()
        dn_in[j] = (wd_v[rows_mine, pl.ds(j * piece, piece)].astype(F32) + dn_in[j].astype(F32)).astype(BF16)
        keep(dn_in.at[j], dn_half.at[j])
    result["u1"].wait_recv()
    res_up1[...] = (block(down_v, 3, 0)[...].astype(F32) + res_up1[...].astype(F32)).astype(BF16)
    result["u3"] = mail.post(res_up1, res_up2.at[0], up)
    result["d1"].wait_recv()
    res_down1[...] = (block(down_v, 1, 1)[...].astype(F32) + res_down1[...].astype(F32)).astype(BF16)
    result["d3"] = mail.post(res_down1, res_down2.at[1], down)
    for half, i in ((0, 0), (1, 0), (0, 1), (1, 1)):
        rows_i = pl.ds(i * size, size)
        swaps[half, i].wait_recv()
        total[pl.ds(half * rows + i * size, size), :] = stage[half, rows_i, :].astype(F32) + other[
            half, rows_i, :
        ].astype(F32)
    next(rings[0])
    next(rings[1])
    next(rings[2])
    for name in ("u2", "d2", "u3", "d3"):
        result[name].wait_recv()
    for half in range(2):
        value = block(down_v, 0, half)[...].astype(F32) + res_up2[half].astype(F32) + res_down2[half].astype(F32)
        result_sum[pl.ds(half * rows, rows), :] = value.astype(BF16)
    for copy in kept:
        if copy is not None:
            copy.wait()
    mail.finish()


def back_kernel(
    total,
    middle,
    cot,
    gains,
    tok,
    normed,
    query,
    kv_a,
    kv_b,
    logs,
    attended,
    tables,
    turned_a,
    turned_b,
    w_in,
    w_out,
    gu,
    dn,
    result_sum,
    gu_out,
    dn_out,
    in_out,
    wo_out,
    grad_out,
    result_out,
    small_out,
    middle_v,
    cot_v,
    tok_v,
    normed_v,
    query_v,
    kva,
    kvb,
    attended_v,
    turned_a_v,
    turned_b_v,
    w_in_v,
    w_out_v,
    gu_v,
    dn_v,
    down_v,
    gain_rows,
    grad_middle,
    grad_low,
    grad_att,
    flat,
    keys_t,
    dkv_a,
    dkv_b,
    low_kv,
    own_kv,
    from_own,
    from_near,
    grad_pre,
    grad_part,
    grad_in,
    part_in,
    rows_out,
    result_rows,
    gu_n,
    gu_s,
    dn_up1,
    dn_down1,
    dn_up2,
    dn_down2,
    dn_y,
    dn_n,
    dn_s,
    in_p,
    in_t,
    in_up1,
    in_down1,
    in_up2,
    in_down2,
    in_s,
    in_n,
    in_z,
    wo_p,
    wo_t,
    wo_up1,
    wo_down1,
    wo_up2,
    wo_down2,
    wo_s,
    wo_n,
    wo_z,
    bias_own,
    gains_own,
    bias_in,
    gains_in,
    small_a,
    small_b,
    small_t,
    small_n,
    send,
    recv,
    local,
):
    place = here()
    dp, row, col = place
    core = dp % 2
    z = dp // Z_STEP
    twin, near, pair = twin_of(place), near_of(place), pair_of(place)
    up, down, far_z = along_z(place, 1), along_z(place, 3), along_z(place, 2)
    right, left = along_y(place, 1), along_y(place, 3)
    meet(
        [along_y(place, s) for s in (1, 2, 3)]
        + [near_of(place, (row + s) % 4) for s in range(4)]
        + [pair_of(place, (row + s) % 4) for s in range(4)]
        + [twin, up, down, far_z]
    )
    mail = Mail(send, recv)
    kept, arrivals = [], []

    def keep(source, target):
        kept.append(pltpu.make_async_copy(source, target, local.at[len(kept)]))
        kept[-1].start()
        return len(kept) - 1

    def kept_wait(index):
        kept[index].wait()
        kept[index] = None

    def even(start, size):
        return pl.ds(pl.multiple_of(start, 16), size)

    def plus(*values):
        result = values[0].astype(F32)
        for value in values[1:]:
            result = result + value.astype(F32)
        return result

    def dot_nt(left, right):
        return lax.dot_general(left, right, (((1,), (1,)), ((), ())), preferred_element_type=F32)

    rows = tok.shape[0] // 2
    width = tok.shape[1]
    piece = width // 4
    spot = even(row * rows, rows)
    own_rows, other_rows = even(col * rows, rows), even((1 - col) * rows, rows)

    def ffn_flow(i):
        if i < 3:
            height = gu.shape[0] // 3
            start = i * height
            theirs, done = gu_n.at[i], gu_s.at[i]
            mine = gu_v.at[pl.ds(start, height), :]
            swap = mail.post(gu.at[pl.ds(start, height), :], theirs, near)
            half = height // 2
            yield
            if i == 0:
                kept_wait(loads["gu"])
        else:
            height = dn.shape[1]
            start, mine, theirs, done = 0, dn_y, dn_n, dn_s
            half = height // 2
            low, high = pl.ds(start, half), pl.ds(start + half, half)
            first = (mail.post(dn.at[2, low, :], dn_up1, right), mail.post(dn.at[2, high, :], dn_down1, left))
            straight = (
                mail.post(dn.at[1, high, :], dn_up2.at[pl.ds(half, half), :], right),
                mail.post(dn.at[3, low, :], dn_down2.at[pl.ds(0, half), :], left),
            )
            yield
            kept_wait(loads["dn"])
            first[0].wait_recv()
            dn_up1[...] = plus(dn_v[1, low, :], dn_up1[...]).astype(BF16)
            last = [mail.post(dn_up1, dn_up2.at[pl.ds(0, half), :], right)]
            first[1].wait_recv()
            dn_down1[...] = plus(dn_v[3, high, :], dn_down1[...]).astype(BF16)
            last.append(mail.post(dn_down1, dn_down2.at[pl.ds(half, half), :], left))
            yield
            for copy in straight + tuple(last):
                copy.wait_recv()
            mine[...] = plus(dn_v[0], dn_up2[...], dn_down2[...]).astype(BF16)
            swap = mail.post(mine, theirs, near)
            yield
        swap.wait_recv()
        done[...] = plus(mine[...], theirs[...]).astype(BF16)

        def room(slot, which=None):
            begin, size = (start, height) if which is None else (start + which * half, half)
            if i < 3:
                share = gu_out.shape[2] // 4
                lanes = pl.ds(pl.multiple_of(slot * share, LANES), share)
                return gu_out.at[core, pl.ds(begin, size), lanes]
            return dn_out.at[even((slot * 2 + core) * height + begin, size), :]

        posts = {}
        for turn in range(2):
            for name, device, which in (("u", up, turn), ("d", down, 1 - turn)):
                posts[name, which] = mail.post(done.at[pl.ds(which * half, half), :], room(z, which), device)
        keep(done, room(z))
        arrivals.append(mail.post(done, room(z), twin))
        yield
        posts["u", 0].wait_recv()
        block = room((z + 3) % 4, 0)
        one_more = mail.post(block, block, up)
        posts["d", 1].wait_recv()
        block = room((z + 1) % 4, 1)
        two_more = mail.post(block, block, down)
        yield
        posts["u", 1].wait_recv()
        block = room((z + 3) % 4)
        arrivals.append(mail.post(block, block, twin))
        posts["d", 0].wait_recv()
        block = room((z + 1) % 4)
        arrivals.append(mail.post(block, block, twin))
        one_more.wait_recv()
        two_more.wait_recv()
        block = room((z + 2) % 4)
        arrivals.append(mail.post(block, block, twin))
        yield

    def weight_flow(part, t, up1, down1, up2, down2, total_h, theirs, quarter, out):
        height = t.shape[1]
        half = height // 2
        low, high = pl.ds(0, half), pl.ds(half, half)
        copy = mail.post(part.at[:, even((1 - core) * height, height), :], t, twin)
        yield
        copy.wait_recv()
        for j in range(4):
            t[j] = plus(part[j, even(core * height, height), :], t[j]).astype(BF16)
        first = (mail.post(t.at[2, low, :], up1, right), mail.post(t.at[2, high, :], down1, left))
        straight = (
            mail.post(t.at[1, high, :], up2.at[high, :], right),
            mail.post(t.at[3, low, :], down2.at[low, :], left),
        )
        yield
        first[0].wait_recv()
        up1[...] = plus(t[1, low, :], up1[...]).astype(BF16)
        last = [mail.post(up1, up2.at[low, :], right)]
        first[1].wait_recv()
        down1[...] = plus(t[3, high, :], down1[...]).astype(BF16)
        last.append(mail.post(down1, down2.at[high, :], left))
        yield
        for copy in straight + tuple(last):
            copy.wait_recv()
        total_h[...] = plus(t[0], up2[...], down2[...]).astype(BF16)
        swap = mail.post(total_h, theirs, near)
        yield
        swap.wait_recv()
        t[0] = plus(total_h[...], theirs[...]).astype(BF16)
        size = height // 4
        copies = []
        for step, device in ((1, up), (3, down), (2, far_z)):
            source = t.at[0, even(((z + step) % 4) * size, size), :]
            copies.append(mail.post(source, quarter.at[step - 1], device))
        yield
        for copy in copies:
            copy.wait_recv()
        mine = even(z * size, size)
        theirs[0:size, :] = plus(t[0, mine, :], quarter[0], quarter[1], quarter[2]).astype(BF16)
        place_of = lambda owner: out.at[even(core * height + owner * size, size), :]
        copies = [mail.post(theirs.at[0:size, :], place_of(z), device) for device in (up, down, far_z)]
        arrivals.append(mail.post(theirs.at[0:size, :], place_of(z), twin))
        keep(theirs.at[0:size, :], place_of(z))
        yield
        for copy in copies:
            copy.wait_recv()
        for step in (1, 2, 3):
            block = place_of((z + step) % 4)
            arrivals.append(mail.post(block, block, twin))
        yield

    def result_flow():
        swap = mail.post(result_sum.at[other_rows, :], part_in, pair)
        yield
        kept_wait(loads["down"])
        swap.wait_recv()
        result_rows[...] = (middle_v[own_rows, :] + plus(down_v[own_rows, :], part_in[...])).astype(BF16)
        yield
        spread(result_rows, result_out)
        yield

    def spread(source, target):
        for step in range(4):
            lanes = pl.ds(step * piece, piece)
            if step:
                arrivals.append(mail.post(source.at[:, lanes], target.at[spot, :], along_y(place, step)))
            else:
                keep(source.at[:, lanes], target.at[spot, :])

    flows = [ffn_flow(i) for i in range(4)]
    loads = {}
    for name, source, target in (
        ("middle", middle, middle_v),
        ("cot", cot.at[0], cot_v),
        ("w_out", w_out, w_out_v),
        ("attended", attended, attended_v),
        ("query", query, query_v),
        ("kva", kv_a, kva),
        ("kvb", kv_b, kvb),
        ("ta", turned_a, turned_a_v),
        ("tb", turned_b, turned_b_v),
        ("gu", gu, gu_v),
        ("w_in", w_in, w_in_v),
        ("normed", normed, normed_v),
        ("tok", tok, tok_v),
        ("dn", dn, dn_v),
        ("down", result_sum, down_v),
    ):
        loads[name] = keep(source, target)
    result_steps = result_flow()
    for j in range(4):
        gain_rows[:, j * piece : (j + 1) * piece] = gains[j]

    def norm_back(stream, gain, incoming):
        scale = lax.rsqrt(jnp.sum(stream * stream, -1, keepdims=True) * (1.0 / width) + EPS)
        scaled = incoming * gain
        inner = jnp.sum(scaled * stream, -1, keepdims=True) * (1.0 / width)
        back = scale * scaled - stream * (scale * scale * scale * inner)
        return back, jnp.sum(incoming * stream * scale, 0, keepdims=True)

    kept_wait(loads["middle"])
    kept_wait(loads["cot"])
    gain_ffn_part = jnp.zeros((1, width), F32)
    for half in range(2):
        part = slice(half * rows, (half + 1) * rows)
        back, gain_part = norm_back(middle_v[part, :], gain_rows[1:2, :], total[part, :])
        value = cot_v[part, :].astype(F32) + back
        grad_middle[part, :] = value
        grad_low[part, :] = value.astype(BF16)
        gain_ffn_part = gain_ffn_part + gain_part
    gains_own[...] = jnp.zeros_like(gains_own)
    for j in range(4):
        gains_own[j, 1:2, :] = 0.5 * gain_ffn_part[:, j * piece : (j + 1) * piece]
    next(flows[0])
    next(flows[3])
    kept_wait(loads["w_out"])
    q_width = w_out.shape[0]
    for first in range(0, q_width, 256):
        lanes = slice(first, first + 256)
        grad_att[:, lanes] = dot_nt(grad_low[...], w_out_v[lanes, :]).astype(BF16)

    def turn_over(source, target, count):
        for t in range(count):
            lanes = slice(t * LANES, (t + 1) * LANES)
            target[lanes, 0 : source.shape[0]] = source[:, lanes].T

    kept_wait(loads["attended"])
    turn_over(attended_v, flat, q_width // LANES)
    for j in range(4):
        wo_p[j] = jnp.dot(
            flat[0:q_width, :], grad_low[:, j * piece : (j + 1) * piece], preferred_element_type=F32
        ).astype(BF16)
    wo_steps = weight_flow(wo_p, wo_t, wo_up1, wo_down1, wo_up2, wo_down2, wo_s, wo_n, wo_z, wo_out)

    for name in ("query", "kva", "kvb", "ta", "tb"):
        kept_wait(loads[name])
    heads = q_width // HEAD_SIZE
    factor = HEAD_SIZE ** (-0.5)

    def unrotate(value, half):
        part = slice(half * rows, (half + 1) * rows)
        return value * tables[0, part, :] + pltpu.roll(value * tables[1, part, :], HEAD_SIZE // 2, 1)

    def attend_back(half, keys, mask, sums):
        part = slice(half * rows, (half + 1) * rows)
        count = keys.shape[0]
        for t in range(count // LANES):
            lanes = slice(t * LANES, (t + 1) * LANES)
            keys_t[:, lanes] = keys[lanes, 0:HEAD_SIZE].T
        sums[...] = jnp.zeros_like(sums)

        @pl.loop(0, heads)
        def _(h):
            lanes = pl.ds(pl.multiple_of(h * HEAD_SIZE, LANES), HEAD_SIZE)
            one, grad = query_v[part, lanes], grad_att[part, lanes]
            raw = dot_nt(keys[:, 0:HEAD_SIZE], one)
            probs = jnp.exp(raw * factor + mask[...] - logs[half * heads + h, 0:1, :])
            grad_probs = dot_nt(keys[:, HEAD_SIZE : 2 * HEAD_SIZE], grad)
            inner = jnp.sum(grad_probs * probs, 0, keepdims=True)
            grad_scores = (probs * (grad_probs - inner)).astype(BF16)
            sums[:, 0:HEAD_SIZE] += jnp.dot(grad_scores, one, preferred_element_type=F32)
            sums[:, HEAD_SIZE : 2 * HEAD_SIZE] += jnp.dot(probs.astype(BF16), grad, preferred_element_type=F32)
            grad_query = jnp.dot(keys_t[:, 0:count], grad_scores, preferred_element_type=F32).T * factor
            grad_pre[part, lanes] = unrotate(grad_query, half).astype(BF16)

    def low_sums(sums, part):
        return (sums[part, 0:HEAD_SIZE] * factor).astype(BF16), sums[part, HEAD_SIZE : 2 * HEAD_SIZE].astype(BF16)

    next(flows[1])
    attend_back(1, kvb, turned_b_v, dkv_b)
    half_rows = kva.shape[0]
    low_part, high_part = slice(0, half_rows), slice(half_rows, 2 * half_rows)
    for target, sums, part in ((low_kv, dkv_b, low_part), (own_kv.at[1], dkv_b, high_part)):
        target[:, 0:HEAD_SIZE], target[:, HEAD_SIZE : 2 * HEAD_SIZE] = low_sums(sums, part)
    kv_got = []
    for step in range(4):
        other = (row + step) % 4
        part = even(other * rows, rows)
        kv_got.append(mail.post(low_kv.at[part, :], from_near.at[step], near_of(place, other)))
        if step:
            kv_got.append(mail.post(own_kv.at[1, part, :], from_own.at[step - 1, 1], along_y(place, step)))
    next(flows[0])
    attend_back(0, kva, turned_a_v, dkv_a)
    target = own_kv.at[0]
    target[:, 0:HEAD_SIZE], target[:, HEAD_SIZE : 2 * HEAD_SIZE] = low_sums(dkv_a, low_part)
    for step in (1, 2, 3):
        part = even(((row + step) % 4) * rows, rows)
        kv_got.append(mail.post(own_kv.at[0, part, :], from_own.at[step - 1, 0], along_y(place, step)))
    next(result_steps)
    next(flows[3])
    next(flows[0])
    next(wo_steps)
    next(flows[2])
    kept_wait(loads["normed"])
    turn_over(normed_v, flat, width // LANES)
    next(flows[1])
    for copy in kv_got:
        copy.wait_recv()
    for half in range(2):
        part = slice(half * rows, (half + 1) * rows)
        value = own_kv[half, spot, :].astype(F32)
        for step in range(3):
            value = value + from_own[step, half].astype(F32)
        if half == 0:
            for step in range(4):
                value = value + from_near[step].astype(F32)
        grad_pre[part, q_width : q_width + HEAD_SIZE] = unrotate(value[:, 0:HEAD_SIZE], half).astype(BF16)
        grad_pre[part, q_width + HEAD_SIZE : q_width + 2 * HEAD_SIZE] = value[:, HEAD_SIZE : 2 * HEAD_SIZE].astype(
            BF16
        )
    next(wo_steps)
    kept_wait(loads["w_in"])
    for j in range(4):
        grad_part[:, j * piece : (j + 1) * piece] = dot_nt(grad_pre[...], w_in_v[j]).astype(BF16)
    swap = mail.post(grad_part.at[other_rows, :], grad_in, pair)
    for j in range(4):
        in_p[j] = jnp.dot(flat[j * piece : (j + 1) * piece, :], grad_pre[...], preferred_element_type=F32).astype(BF16)
    in_steps = weight_flow(in_p, in_t, in_up1, in_down1, in_up2, in_down2, in_s, in_n, in_z, in_out)
    next(flows[3])
    next(flows[2])
    next(flows[1])
    next(wo_steps)
    next(in_steps)
    next(in_steps)
    next(flows[3])
    next(wo_steps)
    bias_own[...] = jnp.zeros_like(bias_own)
    bias_own[0:1, :] = jnp.sum(grad_pre[...].astype(F32), 0, keepdims=True)
    next(in_steps)
    kept_wait(loads["tok"])
    swap.wait_recv()
    back, gain_part = norm_back(
        tok_v[own_rows, :].astype(F32), gain_rows[0:1, :], plus(grad_part[own_rows, :], grad_in[...])
    )
    rows_out[...] = (grad_middle[own_rows, :] + back).astype(BF16)
    for j in range(4):
        gains_own[j, 0:1, :] = gain_part[:, j * piece : (j + 1) * piece]
    next(result_steps)
    next(wo_steps)
    next(in_steps)
    next(flows[0])
    next(flows[2])
    next(wo_steps)
    next(result_steps)
    small_copies, small_kept = [], []
    for step in range(4):
        device = along_y(place, step)
        mine = gains_in.at[col * 4 + row]
        if step:
            small_copies.append(mail.post(bias_own, bias_in.at[row], device))
            small_copies.append(mail.post(gains_own.at[step], mine, device))
        else:
            small_kept.append(keep(bias_own, bias_in.at[row]))
            small_kept.append(keep(gains_own.at[step], mine))
        small_copies.append(mail.post(gains_own.at[step], mine, pair_of(place, (row + step) % 4)))
    spread(rows_out, grad_out)
    next(flows[3])
    next(in_steps)
    for copy in small_copies:
        copy.wait_recv()
    for index in small_kept:
        kept_wait(index)
    small_a[...] = jnp.zeros_like(small_a)
    small_a[0:8, :] = bias_in[0] + bias_in[1] + bias_in[2] + bias_in[3]
    small_a[8:16, 0:piece] = (
        gains_in[0] + gains_in[1] + gains_in[2] + gains_in[3] + gains_in[4] + gains_in[5] + gains_in[6] + gains_in[7]
    )
    small_first = mail.post(small_a, small_t, twin)
    next(flows[1])
    next(wo_steps)
    next(in_steps)
    small_first.wait_recv()
    small_b[...] = small_a[...] + small_t[...]
    small_second = mail.post(small_b, small_n, near)
    small_second.wait_recv()
    small_t[...] = small_b[...] + small_n[...]
    for device in (up, down, far_z):
        arrivals.append(mail.post(small_t, small_out.at[z], device))
    keep(small_t, small_out.at[z])
    for steps in [*flows, wo_steps, in_steps, result_steps]:
        for _ in steps:
            pass
    for copy in arrivals:
        copy.wait_recv()
    for copy in kept:
        if copy is not None:
            copy.wait()
    mail.finish()


def widen_kernel(gate_up, down, w_in, w_out, result, tokens, small, *outs):
    result_w, tokens_w, query_w, key_w, value_w, out_w, gate_w, up_w, down_w, *flat = outs
    total = small[0] + small[1] + small[2] + small[3]
    start = 0
    for line, out in zip((0, 0, 0, 8, 9), flat):
        start = 0 if line else start
        out[...] = total[line, start : start + out.shape[0]]
        start += out.shape[0]
    result_w[...] = result[...].astype(F32)
    tokens_w[...] = tokens[...].astype(F32)
    first, second = query_w.shape[1], query_w.shape[1] + key_w.shape[1]
    query_w[...] = w_in[:, :first].astype(F32)
    key_w[...] = w_in[:, first:second].astype(F32)
    value_w[...] = w_in[:, second:].astype(F32)
    out_w[...] = w_out[...].astype(F32)
    gate_w[...] = gate_up[0, :, : gate_w.shape[1]].astype(F32)
    up_w[...] = gate_up[1, :, : up_w.shape[1]].astype(F32)
    down_w[...] = down[...].astype(F32)


def on_device(
    tokens,
    cotangent,
    lengths,
    gain_attn,
    w_query,
    key_projection,
    value_projection,
    bias_query,
    key_bias_vector,
    value_bias_vector,
    w_out,
    gain_ffn,
    w_gate,
    w_up,
    w_down,
):
    half_rows, piece = tokens.shape
    width = 4 * piece
    rows = half_rows // 4
    q_width = w_query.shape[1]
    kv_width = key_projection.shape[1]
    heads = q_width // HEAD_SIZE
    hidden = w_gate.shape[1]
    share = -(-hidden // (4 * LANES)) * LANES

    in_width = q_width + 2 * kv_width
    thin = piece // 2
    (
        tok_rows,
        cot_full,
        gains4,
        normed,
        query,
        kv_a,
        kv_b,
        logs,
        attended,
        tables,
        middle,
        mask_a,
        mask_b,
        normed_ffn,
        w_in_full,
        w_out_full,
        w_gu_full,
        w_down_full,
    ) = talk(
        front_kernel,
        0,
        FRONT_COPIES,
        FRONT_LOCAL,
        [
            ((2 * rows, width), BF16),
            ((4, 2 * rows, width), BF16),
            ((4, 8, piece), F32),
            ((2 * rows, width), BF16),
            ((2 * rows, q_width), BF16),
            ((half_rows, 2 * kv_width), BF16),
            ((2 * half_rows, 2 * kv_width), BF16),
            ((2 * heads, 8, rows), F32),
            ((2 * rows, q_width), BF16),
            ((2, 2 * rows, HEAD_SIZE), F32),
            ((2 * rows, width), F32),
            ((half_rows, rows), F32),
            ((2 * half_rows, rows), F32),
            ((2 * rows, width), BF16),
            ((4, piece, in_width), BF16),
            ((q_width, width), BF16),
            ((4, 2, thin, 2 * share), BF16),
            ((share, width), BF16),
        ],
        [ANY] * 2 + [VMEM] * 6 + [ANY] * 7,
        [ANY] * 3 + [VMEM] * 2 + [ANY] * 2 + [VMEM] * 7 + [ANY] * 4,
        [
            pltpu.VMEM((8, LANES), jnp.int32),
            pltpu.VMEM((8, piece), F32),
            pltpu.VMEM((2 * rows, width), BF16),
            pltpu.VMEM((2, 8, LANES), jnp.int32),
            pltpu.VMEM((4, 8, piece), F32),
            pltpu.VMEM((4, piece, in_width), BF16),
            pltpu.VMEM((q_width, width), BF16),
            pltpu.VMEM((2, thin, 2 * share), BF16),
            pltpu.VMEM((share, piece), BF16),
            pltpu.VMEM((thin, LANES), BF16),
            pltpu.VMEM((LANES, piece), BF16),
            pltpu.VMEM((2 * rows, 2 * kv_width), BF16),
            pltpu.VMEM((half_rows, 2 * kv_width), BF16),
            pltpu.VMEM((2 * half_rows, 2 * kv_width), BF16),
            pltpu.VMEM((rows, half_rows), F32),
            pltpu.VMEM((rows, 2 * half_rows), F32),
            pltpu.VMEM((2 * rows, width), BF16),
            pltpu.VMEM((2 * rows, width), BF16),
        ],
        limit=56,
    )(
        tokens,
        cotangent,
        lengths,
        gain_attn,
        gain_ffn,
        bias_query,
        key_bias_vector,
        value_bias_vector,
        w_query,
        key_projection,
        value_projection,
        w_out,
        w_gate,
        w_up,
        w_down,
    )

    w_both_full = w_gu_full.reshape(width, 2 * share)
    half_block = (2, rows, width)
    grad_normed_ffn, both_sum, down_half, result_sum = talk(
        ffn_kernel,
        4,
        52,
        14,
        [
            ((2 * rows, width), F32),
            ((piece, share), BF16),
            ((4, share // 2, piece), BF16),
            ((2 * rows, width), BF16),
        ],
        [ANY] * 4,
        [VMEM, VMEM, ANY, VMEM],
        [
            pltpu.VMEM(shape, BF16)
            for shape in (
                (8 * rows, width),
                (8 * rows, width),
                (width, 2 * share),
                (share, width),
                (8 * rows, 2 * share),
                (8 * rows, share),
                (8 * rows, width),
                (width, 8 * rows),
                (8 * rows, width),
                (4, piece, share),
                (4, share // 2, piece),
                (2, rows // 2, width),
                (2, rows // 2, width),
                half_block,
                half_block,
                half_block,
                (2, rows // 2, width),
                (2, rows // 2, width),
                half_block,
                (rows, width),
                (rows, width),
                half_block,
                half_block,
                (3, piece // 6, share),
                (3, piece // 6, share),
                (3, piece // 3, share),
                (3, piece // 3, share),
            )
        ],
        limit=60,
    )(normed_ffn, cot_full, w_both_full, w_down_full)
    thirds = piece // 3
    q_half, w_half = (thin, in_width), (q_width // 2, piece)
    gu_chunk, dn_chunk = (3, thirds, share), (share // 2, piece)

    def halved(shape):
        return (*shape[:-2], shape[-2] // 2, shape[-1])

    def weight_scratch(shape):
        return [
            (4, 2 * shape[0], shape[1]),
            (4, *shape),
            halved(shape),
            halved(shape),
            shape,
            shape,
            shape,
            shape,
            (3, shape[0] // 4, shape[1]),
        ]

    def scratch(kind, *shapes):
        return [pltpu.VMEM(shape, kind) for shape in shapes]

    gate_up, down_all, in_total, out_total, grad_tokens, result, small_all = talk(
        back_kernel,
        8,
        BACK_COPIES,
        BACK_LOCAL,
        [
            ((2, piece, 4 * share), BF16),
            ((4 * share, piece), BF16),
            ((piece, in_width), BF16),
            ((q_width, piece), BF16),
            ((half_rows, piece), BF16),
            ((half_rows, piece), BF16),
            ((4, 16, in_width), F32),
        ],
        [VMEM, ANY, ANY, VMEM] + [ANY] * 5 + [VMEM, ANY, VMEM] + [ANY] * 7,
        [ANY] * 7,
        scratch(F32, (2 * rows, width))
        + scratch(
            BF16,
            (2 * rows, width),
            (2 * rows, width),
            (2 * rows, width),
            (2 * rows, q_width),
            (half_rows, 2 * kv_width),
            (2 * half_rows, 2 * kv_width),
            (2 * rows, q_width),
        )
        + scratch(F32, (half_rows, rows), (2 * half_rows, rows))
        + scratch(
            BF16,
            (4, piece, in_width),
            (q_width, width),
            (piece, share),
            (4, share // 2, piece),
            (2 * rows, width),
        )
        + scratch(F32, (8, width), (2 * rows, width))
        + scratch(BF16, (2 * rows, width), (2 * rows, q_width), (width, 2 * rows), (HEAD_SIZE, 2 * half_rows))
        + scratch(F32, (half_rows, 2 * kv_width), (2 * half_rows, 2 * kv_width))
        + scratch(
            BF16,
            (half_rows, 2 * kv_width),
            (2, half_rows, 2 * kv_width),
            (3, 2, rows, 2 * kv_width),
            (4, rows, 2 * kv_width),
            (2 * rows, in_width),
            (2 * rows, width),
            (rows, width),
            (rows, width),
            (rows, width),
            (rows, width),
            gu_chunk,
            gu_chunk,
            halved(dn_chunk),
            halved(dn_chunk),
            dn_chunk,
            dn_chunk,
            dn_chunk,
            dn_chunk,
            dn_chunk,
            *weight_scratch(q_half),
            *weight_scratch(w_half),
        )
        + scratch(F32, (8, in_width), (4, 8, piece), (4, 8, in_width), (8, 8, piece))
        + scratch(F32, *[(16, in_width)] * 4),
        limit=60,
    )(
        grad_normed_ffn,
        middle,
        cot_full,
        gains4,
        tok_rows,
        normed,
        query,
        kv_a,
        kv_b,
        logs,
        attended,
        tables,
        mask_a,
        mask_b,
        w_in_full,
        w_out_full,
        both_sum,
        down_half,
        result_sum,
    )
    steps = 8
    narrow = [gate_up, down_all, in_total, out_total, result, grad_tokens, small_all]
    lines = [(q_width,), (kv_width,), (kv_width,), (piece,), (piece,)]
    wide = [
        (half_rows, piece),
        (half_rows, piece),
        (piece, q_width),
        (piece, kv_width),
        (piece, kv_width),
        (q_width, piece),
        (piece, hidden),
        (piece, hidden),
        (hidden, piece),
    ]

    def in_block(array):
        if array is small_all:
            return pl.BlockSpec(array.shape, lambda i: (0, 0, 0))
        if array.ndim == 3:
            return pl.BlockSpec((2, array.shape[1] // steps, array.shape[2]), lambda i: (0, i, 0))
        if array is down_all:
            return pl.BlockSpec((hidden // steps, piece), lambda i: (i, 0))
        return pl.BlockSpec((array.shape[0] // steps, array.shape[1]), lambda i: (i, 0))

    wide_out = pl.pallas_call(
        widen_kernel,
        grid=(steps,),
        out_shape=[jax.ShapeDtypeStruct(shape, F32) for shape in wide + lines],
        in_specs=[in_block(array) for array in narrow],
        out_specs=[pl.BlockSpec((shape[0] // steps, shape[1]), lambda i: (i, 0)) for shape in wide]
        + [pl.BlockSpec(shape, lambda i: (0,)) for shape in lines],
        compiler_params=pltpu.CompilerParams(vmem_limit_bytes=60 << 20),
    )(*narrow)
    result_w, tokens_w, query_w, key_w, value_w, out_w, gate_w, up_w, down_w, *flat = wide_out
    bias_q, bias_k, bias_v, gain_one, gain_two = flat
    return (
        result_w,
        tokens_w,
        gain_one,
        query_w,
        key_w,
        value_w,
        bias_q,
        bias_k,
        bias_v,
        out_w,
        gain_two,
        gate_w,
        up_w,
        down_w,
    )


def solution(mesh):
    placed = (
        P(("dp", "col"), "row"),
        P(("dp", "col"), "row"),
        P("dp", None),
        P("row"),
        P("row", "col"),
        P("row", "col"),
        P("row", "col"),
        P("col"),
        P("col"),
        P("col"),
        P("col", "row"),
        P("row"),
        P("row", "col"),
        P("row", "col"),
        P("col", "row"),
    )
    return jax.shard_map(
        on_device,
        mesh=mesh,
        in_specs=placed,
        out_specs=(
            P(("dp", "col"), "row"),
            P(("dp", "col"), "row"),
            P("row"),
            P("row", "col"),
            P("row", "col"),
            P("row", "col"),
            P("col"),
            P("col"),
            P("col"),
            P("col", "row"),
            P("row"),
            P("row", "col"),
            P("row", "col"),
            P("col", "row"),
        ),
        check_vma=False,
    )
```

profile of v0, /device:TPU:1, one launch (start us, length us, event | category | flops | bytes accessed | tf_op | source)
XLA Modules:
  0.0 267.9 jit_solution(785076094152729644)
XLA Ops:
  0.7 81.8 %shard_map.254 = (bf16[256,1536]{1,0:T(8,128)(2,1)}, bf16[4,256,1536]{2,1,0:T(8,128)(2,1)}, f32[4,8,384]{2,1,0:T(8,128)}, bf16[256,1536]{1,0:T(8,128)(2,1)}, bf1...) custom-call(bf16[512,384]{1,0:T(8,128)(2,1)} %tok.1, ...), custom_call_target="tpu_custom_call" | custom-call | tf_op jit(solution)/shard_map/pallas_call | solution.py:1418
  82.4 86.8 %shard_map.255 = (f32[256,1536]{1,0:T(8,128)}, bf16[384,1152]{1,0:T(8,128)(2,1)}, bf16[4,576,384]{2,1,0:T(8,128)(2,1)}, bf16[256,1536]{1,0:T(8,128)(2,1)}) custom-call(bf16[256,1536]{1,0:T(8,128)(2,1)} %get-tuple-element.57.normed, bf16[4,256,1536]{2,1,0:T(8,128)(2,1)} %get-tuple-element.58.cot, bf16[1536,2304]{1,0:T(8,128)(2,1)} %bitcast.1, ...), custom_call_target="tpu_custom_call" | custom-call | tf_op jit(solution)/shard_map/pallas_call | solution.py:1486
  169.2 84.3 %shard_map.256 = (bf16[2,384,4608]{2,1,0:T(8,128)(2,1)}, bf16[4608,384]{1,0:T(8,128)(2,1)}, bf16[384,1024]{1,0:T(8,128)(2,1)}, bf16[768,384]{1,0:T(8,128)(2,1)},...) custom-call(f32[256,1536]{1,0:T(8,128)} %get-tuple-element.61.total, ...), custom_call_target="tpu_custom_call" | custom-call | tf_op jit(solution)/shard_map/pallas_call | solution.py:1556
  253.5 14.2 %shard_map.257 = (f32[512,384]{1,0:T(8,128)}, f32[512,384]{1,0:T(8,128)}, f32[384,768]{1,0:T(8,128)}, f32[384,128]{1,0:T(8,128)}, f32[384,128]{1,0:T(8,128)}, /*...) custom-call(bf16[2,384,4608]{2,1,0:T(8,128)(2,1)} %get-tuple-element, ...), custom_call_target="tpu_custom_call" | custom-call | tf_op jit(solution)/shard_map/pallas_call | solution.py:1667
where the time goes:
time: 272 us; the launch traced here: 268 us
  Pallas kernels  267 us (98%)
    pallas_call x1, Pallas kernels, on_device(): talk(ffn_kernel, 4, 52, 14, [((2 * rows, width), F32), ((piece, share), B...  86.8 us
    pallas_call x1, Pallas kernels, on_device(): talk(back_kernel, 8, BACK_COPIES, BACK_LOCAL, [((2, piece, 4 * share), BF...  84.3 us
    pallas_call x1, Pallas kernels, on_device(): talk(front_kernel, 0, FRONT_COPIES, FRONT_LOCAL, [((2 * rows, width), BF1...  81.8 us
    pallas_call x1, Pallas kernels, on_device(): pl.pallas_call(widen_kernel, grid=(steps,), out_shape=[jax.ShapeDtypeStru...  14.2 us

commit v1 on v0

--- a/solution.py
+++ b/solution.py
@@ -20,8 +20,8 @@
 Z_STEP = 4
 FRONT_COPIES = 77
 FRONT_LOCAL = 27
-BACK_COPIES = 119
-BACK_LOCAL = 26
+BACK_COPIES = 139
+BACK_LOCAL = 27
 
 
 def here():
@@ -445,6 +445,8 @@
     norm_rows(1 - col)
     cot_pair = to_pair(cotangents, cot_full.at[0])
     z_third(in_parts, in_far)
+    y_forward("gu", gu_part)
+    y_share("gu", gu_part, near_gu, near)
     for copy in shares:
         copy.wait_recv()
     shares.clear()
@@ -468,10 +470,6 @@
     a_got, b_got = [], []
     for step in (1, 2, 3):
         a_got.append(mail.post(kv.at[a_rows, :], kva.at[spot, :], along_y(place, step)))
-    for step in range(4):
-        b_got.append(mail.post(kv.at[a_rows, :], kvb.at[spot, :], near_of(place, (row + step) % 4)))
-        if step:
-            b_got.append(mail.post(kv.at[b_rows, :], kvb.at[high_spot, :], along_y(place, step)))
     kva[spot, :] = kv[a_rows, :]
     kvb[high_spot, :] = kv[b_rows, :]
     for first in range(0, q_width, 2 * HEAD_SIZE):
@@ -480,8 +478,6 @@
             lanes = slice(first + i * HEAD_SIZE, first + (i + 1) * HEAD_SIZE)
             query[:, lanes] = rotate(value[:, i * HEAD_SIZE : (i + 1) * HEAD_SIZE]).astype(BF16)
 
-    y_forward("gu", gu_part)
-    y_share("gu", gu_part, near_gu, near)
     out_far = z_second(out_side, out_parts, out_z)
     heads = q_width // HEAD_SIZE
     factor = HEAD_SIZE ** (-0.5)
@@ -534,27 +530,31 @@
         copies[1].wait_recv()
         return copies[0], mail.post(target.at[3, part, :], target.at[2, part, :], down)
 
-    cot_pair.wait_recv()
-    cot_z = [z_send(cot_full.at[0], cot_full, half) for half in range(2)]
     for copy in a_got:
         copy.wait_recv()
+    for step in range(4):
+        b_got.append(mail.post(kv.at[a_rows, :], kvb.at[spot, :], near_of(place, (row + step) % 4)))
+        if step:
+            b_got.append(mail.post(kv.at[b_rows, :], kvb.at[high_spot, :], along_y(place, step)))
     keep(kva, kva_out)
     z_third(out_parts, out_far)
     for copy in shares:
         copy.wait_recv()
     keep(w_out, w_out_out)
     swap_a = attend(0, kva, bias_a)
+    cot_pair.wait_recv()
+    cot_z = [z_send(cot_full.at[0], cot_full, half) for half in range(2)]
     for copy in b_got:
         copy.wait_recv()
     keep(kvb, kvb_out)
-    y_start("wd", wd_source, wd_part)
     swap_b = attend(1, kvb, bias_b)
     y_end("gu", gu_part, near_gu, near)
+    y_start("wd", wd_source, wd_part)
     finish_half(0, swap_a)
+    cot_last = [z_forward(cot_full, half, cot_z[half]) for half in range(2)]
     y_forward("wd", wd_part)
-    cot_last = [z_forward(cot_full, half, cot_z[half]) for half in range(2)]
+    finish_half(1, swap_b)
     y_share("wd", wd_part, twins, twin)
-    finish_half(1, swap_b)
     for j, copy in zip((3, 1, 2), near_gu):
         copy.wait_recv()
         twins.append(mail.post(gu_whole(j), gu_whole(j), twin))
@@ -579,6 +579,7 @@
     gu_sum,
     dn_half,
     result_sum,
+    result_ahead,
     x,
     cot_v,
     wgu_v,
@@ -789,14 +790,14 @@
             part = pl.ds(pl.multiple_of(c * 2 * rows, 2 * rows), 2 * rows)
             down_v[part, lanes] = jnp.dot(act[part, :], wd_v[:, lanes], preferred_element_type=F32).astype(BF16)
 
+    settle(0)
+    settle(1)
     result = {
         "u1": mail.post(block(down_v, 2, 0), res_up1, up),
         "d1": mail.post(block(down_v, 2, 1), res_down1, down),
-        "u2": mail.post(block(down_v, 3, 1), res_up2.at[1], up),
-        "d2": mail.post(block(down_v, 1, 0), res_down2.at[0], down),
+        "u2": mail.post(block(down_v, 3, 1), res_up2, up),
+        "d2": mail.post(block(down_v, 1, 0), res_down2, down),
     }
-    settle(0)
-    settle(1)
     turn_over(act, turned)
 
     @pl.loop(0, width // tile)
@@ -818,12 +819,6 @@
         shared[4 + j].wait_recv()
         dn_in[j] = (wd_v[rows_mine, pl.ds(j * piece, piece)].astype(F32) + dn_in[j].astype(F32)).astype(BF16)
         keep(dn_in.at[j], dn_half.at[j])
-    result["u1"].wait_recv()
-    res_up1[...] = (block(down_v, 3, 0)[...].astype(F32) + res_up1[...].astype(F32)).astype(BF16)
-    result["u3"] = mail.post(res_up1, res_up2.at[0], up)
-    result["d1"].wait_recv()
-    res_down1[...] = (block(down_v, 1, 1)[...].astype(F32) + res_down1[...].astype(F32)).astype(BF16)
-    result["d3"] = mail.post(res_down1, res_down2.at[1], down)
     for half, i in ((0, 0), (1, 0), (0, 1), (1, 1)):
         rows_i = pl.ds(i * size, size)
         swaps[half, i].wait_recv()
@@ -833,10 +828,12 @@
     next(rings[0])
     next(rings[1])
     next(rings[2])
-    for name in ("u2", "d2", "u3", "d3"):
-        result[name].wait_recv()
-    for half in range(2):
-        value = block(down_v, 0, half)[...].astype(F32) + res_up2[half].astype(F32) + res_down2[half].astype(F32)
+    for copy in result.values():
+        copy.wait_recv()
+    result_ahead[0] = (block(down_v, 3, 0)[...].astype(F32) + res_up1[...].astype(F32)).astype(BF16)
+    result_ahead[1] = (block(down_v, 1, 1)[...].astype(F32) + res_down1[...].astype(F32)).astype(BF16)
+    for half, theirs in ((0, res_down2), (1, res_up2)):
+        value = block(down_v, 0, half)[...].astype(F32) + theirs[...].astype(F32)
         result_sum[pl.ds(half * rows, rows), :] = value.astype(BF16)
     for copy in kept:
         if copy is not None:
@@ -864,9 +861,11 @@
     gu,
     dn,
     result_sum,
+    ahead,
     gu_out,
     dn_out,
     in_out,
+    kw_out,
     wo_out,
     grad_out,
     result_out,
@@ -922,6 +921,15 @@
     in_s,
     in_n,
     in_z,
+    kw_p,
+    kw_t,
+    kw_up1,
+    kw_down1,
+    kw_up2,
+    kw_down2,
+    kw_s,
+    kw_n,
+    kw_z,
     wo_p,
     wo_t,
     wo_up1,
@@ -931,6 +939,8 @@
     wo_s,
     wo_n,
     wo_z,
+    res_in,
+    res_total,
     bias_own,
     gains_own,
     bias_in,
@@ -965,8 +975,9 @@
         return len(kept) - 1
 
     def kept_wait(index):
-        kept[index].wait()
-        kept[index] = None
+        if kept[index] is not None:
+            kept[index].wait()
+            kept[index] = None
 
     def even(start, size):
         return pl.ds(pl.multiple_of(start, 16), size)
@@ -995,8 +1006,7 @@
             swap = mail.post(gu.at[pl.ds(start, height), :], theirs, near)
             half = height // 2
             yield
-            if i == 0:
-                kept_wait(loads["gu"])
+            kept_wait(loads["gu"])
         else:
             height = dn.shape[1]
             start, mine, theirs, done = 0, dn_y, dn_n, dn_s
@@ -1110,11 +1120,17 @@
         yield
 
     def result_flow():
-        swap = mail.post(result_sum.at[other_rows, :], part_in, pair)
+        copies = (mail.post(ahead.at[0], res_in.at[0], up), mail.post(ahead.at[1], res_in.at[1], down))
         yield
         kept_wait(loads["down"])
+        for half, copy in enumerate(copies):
+            copy.wait_recv()
+            part = pl.ds(half * rows, rows)
+            res_total[part, :] = plus(down_v[part, :], res_in[half]).astype(BF16)
+        swap = mail.post(res_total.at[other_rows, :], part_in, pair)
+        yield
         swap.wait_recv()
-        result_rows[...] = (middle_v[own_rows, :] + plus(down_v[own_rows, :], part_in[...])).astype(BF16)
+        result_rows[...] = (middle_v[own_rows, :] + plus(res_total[own_rows, :], part_in[...])).astype(BF16)
         yield
         spread(result_rows, result_out)
         yield
@@ -1148,6 +1164,7 @@
     ):
         loads[name] = keep(source, target)
     result_steps = result_flow()
+    next(flows[2])
     for j in range(4):
         gain_rows[:, j * piece : (j + 1) * piece] = gains[j]
 
@@ -1171,8 +1188,8 @@
     gains_own[...] = jnp.zeros_like(gains_own)
     for j in range(4):
         gains_own[j, 1:2, :] = 0.5 * gain_ffn_part[:, j * piece : (j + 1) * piece]
-    next(flows[0])
     next(flows[3])
+    next(result_steps)
     kept_wait(loads["w_out"])
     q_width = w_out.shape[0]
     for first in range(0, q_width, 256):
@@ -1191,6 +1208,7 @@
             flat[0:q_width, :], grad_low[:, j * piece : (j + 1) * piece], preferred_element_type=F32
         ).astype(BF16)
     wo_steps = weight_flow(wo_p, wo_t, wo_up1, wo_down1, wo_up2, wo_down2, wo_s, wo_n, wo_z, wo_out)
+    next(flows[0])
 
     for name in ("query", "kva", "kvb", "ta", "tb"):
         kept_wait(loads[name])
@@ -1226,7 +1244,7 @@
     def low_sums(sums, part):
         return (sums[part, 0:HEAD_SIZE] * factor).astype(BF16), sums[part, HEAD_SIZE : 2 * HEAD_SIZE].astype(BF16)
 
-    next(flows[1])
+    next(flows[2])
     attend_back(1, kvb, turned_b_v, dkv_b)
     half_rows = kva.shape[0]
     low_part, high_part = slice(0, half_rows), slice(half_rows, 2 * half_rows)
@@ -1239,21 +1257,29 @@
         kv_got.append(mail.post(low_kv.at[part, :], from_near.at[step], near_of(place, other)))
         if step:
             kv_got.append(mail.post(own_kv.at[1, part, :], from_own.at[step - 1, 1], along_y(place, step)))
-    next(flows[0])
     attend_back(0, kva, turned_a_v, dkv_a)
     target = own_kv.at[0]
     target[:, 0:HEAD_SIZE], target[:, HEAD_SIZE : 2 * HEAD_SIZE] = low_sums(dkv_a, low_part)
     for step in (1, 2, 3):
         part = even(((row + step) % 4) * rows, rows)
         kv_got.append(mail.post(own_kv.at[0, part, :], from_own.at[step - 1, 0], along_y(place, step)))
+    next(flows[2])
     next(result_steps)
+    next(wo_steps)
     next(flows[3])
+    next(flows[1])
     next(flows[0])
-    next(wo_steps)
-    next(flows[2])
     kept_wait(loads["normed"])
     turn_over(normed_v, flat, width // LANES)
+    for j in range(4):
+        in_p[j] = jnp.dot(
+            flat[j * piece : (j + 1) * piece, :], grad_pre[:, 0:q_width], preferred_element_type=F32
+        ).astype(BF16)
+    in_steps = weight_flow(in_p, in_t, in_up1, in_down1, in_up2, in_down2, in_s, in_n, in_z, in_out)
+    next(wo_steps)
+    next(flows[3])
     next(flows[1])
+    next(flows[0])
     for copy in kv_got:
         copy.wait_recv()
     for half in range(2):
@@ -1268,25 +1294,30 @@
         grad_pre[part, q_width + HEAD_SIZE : q_width + 2 * HEAD_SIZE] = value[:, HEAD_SIZE : 2 * HEAD_SIZE].astype(
             BF16
         )
+    next(in_steps)
     next(wo_steps)
     kept_wait(loads["w_in"])
     for j in range(4):
         grad_part[:, j * piece : (j + 1) * piece] = dot_nt(grad_pre[...], w_in_v[j]).astype(BF16)
     swap = mail.post(grad_part.at[other_rows, :], grad_in, pair)
     for j in range(4):
-        in_p[j] = jnp.dot(flat[j * piece : (j + 1) * piece, :], grad_pre[...], preferred_element_type=F32).astype(BF16)
-    in_steps = weight_flow(in_p, in_t, in_up1, in_down1, in_up2, in_down2, in_s, in_n, in_z, in_out)
-    next(flows[3])
-    next(flows[2])
-    next(flows[1])
-    next(wo_steps)
-    next(in_steps)
+        kw_p[j] = jnp.dot(
+            flat[j * piece : (j + 1) * piece, :], grad_pre[:, q_width:], preferred_element_type=F32
+        ).astype(BF16)
+    kw_steps = weight_flow(kw_p, kw_t, kw_up1, kw_down1, kw_up2, kw_down2, kw_s, kw_n, kw_z, kw_out)
     next(in_steps)
     next(flows[3])
+    next(kw_steps)
     next(wo_steps)
     bias_own[...] = jnp.zeros_like(bias_own)
     bias_own[0:1, :] = jnp.sum(grad_pre[...].astype(F32), 0, keepdims=True)
     next(in_steps)
+    next(wo_steps)
+    next(in_steps)
+    next(flows[1])
+    next(kw_steps)
+    next(wo_steps)
+    next(kw_steps)
     kept_wait(loads["tok"])
     swap.wait_recv()
     back, gain_part = norm_back(
@@ -1296,12 +1327,8 @@
     for j in range(4):
         gains_own[j, 0:1, :] = gain_part[:, j * piece : (j + 1) * piece]
     next(result_steps)
-    next(wo_steps)
+    next(kw_steps)
     next(in_steps)
-    next(flows[0])
-    next(flows[2])
-    next(wo_steps)
-    next(result_steps)
     small_copies, small_kept = [], []
     for step in range(4):
         device = along_y(place, step)
@@ -1313,9 +1340,12 @@
             small_kept.append(keep(bias_own, bias_in.at[row]))
             small_kept.append(keep(gains_own.at[step], mine))
         small_copies.append(mail.post(gains_own.at[step], mine, pair_of(place, (row + step) % 4)))
-    spread(rows_out, grad_out)
+    next(wo_steps)
+    next(kw_steps)
     next(flows[3])
     next(in_steps)
+    spread(rows_out, grad_out)
+    next(result_steps)
     for copy in small_copies:
         copy.wait_recv()
     for index in small_kept:
@@ -1326,18 +1356,17 @@
         gains_in[0] + gains_in[1] + gains_in[2] + gains_in[3] + gains_in[4] + gains_in[5] + gains_in[6] + gains_in[7]
     )
     small_first = mail.post(small_a, small_t, twin)
-    next(flows[1])
-    next(wo_steps)
-    next(in_steps)
     small_first.wait_recv()
     small_b[...] = small_a[...] + small_t[...]
     small_second = mail.post(small_b, small_n, near)
+    next(in_steps)
+    next(kw_steps)
     small_second.wait_recv()
     small_t[...] = small_b[...] + small_n[...]
     for device in (up, down, far_z):
         arrivals.append(mail.post(small_t, small_out.at[z], device))
     keep(small_t, small_out.at[z])
-    for steps in [*flows, wo_steps, in_steps, result_steps]:
+    for steps in [*flows, wo_steps, in_steps, kw_steps, result_steps]:
         for _ in steps:
             pass
     for copy in arrivals:
@@ -1348,7 +1377,7 @@
     mail.finish()
 
 
-def widen_kernel(gate_up, down, w_in, w_out, result, tokens, small, *outs):
+def widen_kernel(gate_up, down, w_in, w_kv, w_out, result, tokens, small, *outs):
     result_w, tokens_w, query_w, key_w, value_w, out_w, gate_w, up_w, down_w, *flat = outs
     total = small[0] + small[1] + small[2] + small[3]
     start = 0
@@ -1358,10 +1387,9 @@
         start += out.shape[0]
     result_w[...] = result[...].astype(F32)
     tokens_w[...] = tokens[...].astype(F32)
-    first, second = query_w.shape[1], query_w.shape[1] + key_w.shape[1]
-    query_w[...] = w_in[:, :first].astype(F32)
-    key_w[...] = w_in[:, first:second].astype(F32)
-    value_w[...] = w_in[:, second:].astype(F32)
+    query_w[...] = w_in[...].astype(F32)
+    key_w[...] = w_kv[:, : key_w.shape[1]].astype(F32)
+    value_w[...] = w_kv[:, key_w.shape[1] :].astype(F32)
     out_w[...] = w_out[...].astype(F32)
     gate_w[...] = gate_up[0, :, : gate_w.shape[1]].astype(F32)
     up_w[...] = gate_up[1, :, : up_w.shape[1]].astype(F32)
@@ -1483,19 +1511,20 @@
 
     w_both_full = w_gu_full.reshape(width, 2 * share)
     half_block = (2, rows, width)
-    grad_normed_ffn, both_sum, down_half, result_sum = talk(
+    grad_normed_ffn, both_sum, down_half, result_sum, result_ahead = talk(
         ffn_kernel,
         4,
-        52,
+        50,
         14,
         [
             ((2 * rows, width), F32),
             ((piece, share), BF16),
             ((4, share // 2, piece), BF16),
             ((2 * rows, width), BF16),
+            ((2, rows, width), BF16),
         ],
         [ANY] * 4,
-        [VMEM, VMEM, ANY, VMEM],
+        [VMEM, VMEM, ANY, VMEM, VMEM],
         [
             pltpu.VMEM(shape, BF16)
             for shape in (
@@ -1520,8 +1549,8 @@
                 half_block,
                 (rows, width),
                 (rows, width),
-                half_block,
-                half_block,
+                (rows, width),
+                (rows, width),
                 (3, piece // 6, share),
                 (3, piece // 6, share),
                 (3, piece // 3, share),
@@ -1531,7 +1560,7 @@
         limit=60,
     )(normed_ffn, cot_full, w_both_full, w_down_full)
     thirds = piece // 3
-    q_half, w_half = (thin, in_width), (q_width // 2, piece)
+    q_half, w_half = (thin, q_width), (q_width // 2, piece)
     gu_chunk, dn_chunk = (3, thirds, share), (share // 2, piece)
 
     def halved(shape):
@@ -1553,7 +1582,7 @@
     def scratch(kind, *shapes):
         return [pltpu.VMEM(shape, kind) for shape in shapes]
 
-    gate_up, down_all, in_total, out_total, grad_tokens, result, small_all = talk(
+    gate_up, down_all, in_total, kv_total, out_total, grad_tokens, result, small_all = talk(
         back_kernel,
         8,
         BACK_COPIES,
@@ -1561,14 +1590,15 @@
         [
             ((2, piece, 4 * share), BF16),
             ((4 * share, piece), BF16),
-            ((piece, in_width), BF16),
+            ((piece, q_width), BF16),
+            ((piece, 2 * kv_width), BF16),
             ((q_width, piece), BF16),
             ((half_rows, piece), BF16),
             ((half_rows, piece), BF16),
             ((4, 16, in_width), F32),
         ],
-        [VMEM, ANY, ANY, VMEM] + [ANY] * 5 + [VMEM, ANY, VMEM] + [ANY] * 7,
-        [ANY] * 7,
+        [VMEM, ANY, ANY, VMEM] + [ANY] * 5 + [VMEM, ANY, VMEM] + [ANY] * 8,
+        [ANY] * 8,
         scratch(F32, (2 * rows, width))
         + scratch(
             BF16,
@@ -1614,7 +1644,10 @@
             dn_chunk,
             dn_chunk,
             *weight_scratch(q_half),
+            *weight_scratch((thin, 2 * kv_width)),
             *weight_scratch(w_half),
+            (2, rows, width),
+            (2 * rows, width),
         )
         + scratch(F32, (8, in_width), (4, 8, piece), (4, 8, in_width), (8, 8, piece))
         + scratch(F32, *[(16, in_width)] * 4),
@@ -1639,9 +1672,10 @@
         both_sum,
         down_half,
         result_sum,
+        result_ahead,
     )
     steps = 8
-    narrow = [gate_up, down_all, in_total, out_total, result, grad_tokens, small_all]
+    narrow = [gate_up, down_all, in_total, kv_total, out_total, result, grad_tokens, small_all]
     lines = [(q_width,), (kv_width,), (kv_width,), (piece,), (piece,)]
     wide = [
         (half_rows, piece),

time: 272 us -> 283 us (1.040)
  Pallas kernels: 267 us -> 278 us
    pallas_call x1, Pallas kernels: 84.3 us -> 91.8 us  [on_device(): talk(back_kernel, 8, BACK_COPIES, BACK_LOCAL, [((2, piece, 4 * share), BF...]
    pallas_call x1, Pallas kernels: 81.8 us -> 88.6 us  [on_device(): talk(front_kernel, 0, FRONT_COPIES, FRONT_LOCAL, [((2 * rows, width), BF1...]
    pallas_call x1, Pallas kernels: 86.8 us -> 83.2 us  [on_device(): talk(ffn_kernel, 4, 50, 14, [((2 * rows, width), F32), ((piece, share), B...]
where the time goes in v1:
time: 283 us; the launch traced here: 279 us
  Pallas kernels  278 us (98%)
    pallas_call x1, Pallas kernels, on_device(): talk(back_kernel, 8, BACK_COPIES, BACK_LOCAL, [((2, piece, 4 * share), BF...  91.8 us
    pallas_call x1, Pallas kernels, on_device(): talk(front_kernel, 0, FRONT_COPIES, FRONT_LOCAL, [((2 * rows, width), BF1...  88.6 us
    pallas_call x1, Pallas kernels, on_device(): talk(ffn_kernel, 4, 50, 14, [((2 * rows, width), F32), ((piece, share), B...  83.2 us
    pallas_call x1, Pallas kernels, on_device(): pl.pallas_call(widen_kernel, grid=(steps,), out_shape=[jax.ShapeDtypeStru...  14.1 us

profile of v1, /device:TPU:1, one launch (start us, length us, event | category | flops | bytes accessed | tf_op | source)
XLA Modules:
  0.0 278.6 jit_solution(1433820394461411620)
XLA Ops:
  0.7 88.6 %shard_map.254 = (bf16[256,1536]{1,0:T(8,128)(2,1)}, bf16[4,256,1536]{2,1,0:T(8,128)(2,1)}, f32[4,8,384]{2,1,0:T(8,128)}, bf16[256,1536]{1,0:T(8,128)(2,1)}, bf1...) custom-call(bf16[512,384]{1,0:T(8,128)(2,1)} %tok.1, ...), custom_call_target="tpu_custom_call" | custom-call | tf_op jit(solution)/shard_map/pallas_call | solution.py:1446
  89.3 83.2 %shard_map.255 = (f32[256,1536]{1,0:T(8,128)}, bf16[384,1152]{1,0:T(8,128)(2,1)}, bf16[4,576,384]{2,1,0:T(8,128)(2,1)}, bf16[256,1536]{1,0:T(8,128)(2,1)}, bf16[2,128,1536]{2,1,0:T(8,128)(2,1)}) custom-call(bf16[256,1536]{1,0:T(8,128)(2,1)} %get-tuple-element.59.normed, bf16[4,256,1536]{2,1,0:T(8,128)(2,1)} %get-tuple-element.60.cot, ...), custom_call_target="tpu_custom_call" | custom-call | tf_op jit(solution)/shard_map/pallas_call | solution.py:1514
  172.5 91.8 %shard_map.256 = (bf16[2,384,4608]{2,1,0:T(8,128)(2,1)}, bf16[4608,384]{1,0:T(8,128)(2,1)}, bf16[384,768]{1,0:T(8,128)(2,1)}, bf16[384,256]{1,0:T(8,128)(2,1)}, ...) custom-call(f32[256,1536]{1,0:T(8,128)} %get-tuple-element.63.total, ...), custom_call_target="tpu_custom_call" | custom-call | tf_op jit(solution)/shard_map/pallas_call | solution.py:1585
  264.3 14.1 %shard_map.257 = (f32[512,384]{1,0:T(8,128)}, f32[512,384]{1,0:T(8,128)}, f32[384,768]{1,0:T(8,128)}, f32[384,128]{1,0:T(8,128)}, f32[384,128]{1,0:T(8,128)}, /*...) custom-call(bf16[2,384,4608]{2,1,0:T(8,128)(2,1)} %get-tuple-element, ...), custom_call_target="tpu_custom_call" | custom-call | tf_op jit(solution)/shard_map/pallas_call | solution.py:1701

commit v2 on v1

--- a/solution.py
+++ b/solution.py
@@ -20,8 +20,8 @@
 Z_STEP = 4
 FRONT_COPIES = 77
 FRONT_LOCAL = 27
-BACK_COPIES = 139
-BACK_LOCAL = 27
+BACK_COPIES = 145
+BACK_LOCAL = 28
 
 
 def here():
@@ -445,8 +445,6 @@
     norm_rows(1 - col)
     cot_pair = to_pair(cotangents, cot_full.at[0])
     z_third(in_parts, in_far)
-    y_forward("gu", gu_part)
-    y_share("gu", gu_part, near_gu, near)
     for copy in shares:
         copy.wait_recv()
     shares.clear()
@@ -478,6 +476,8 @@
             lanes = slice(first + i * HEAD_SIZE, first + (i + 1) * HEAD_SIZE)
             query[:, lanes] = rotate(value[:, i * HEAD_SIZE : (i + 1) * HEAD_SIZE]).astype(BF16)
 
+    y_forward("gu", gu_part)
+    y_share("gu", gu_part, near_gu, near)
     out_far = z_second(out_side, out_parts, out_z)
     heads = q_width // HEAD_SIZE
     factor = HEAD_SIZE ** (-0.5)
@@ -577,6 +577,7 @@
     wd,
     total,
     gu_sum,
+    gu_late,
     dn_half,
     result_sum,
     result_ahead,
@@ -779,7 +780,8 @@
         gu_sum[part, :] = value.astype(BF16)
         yield
 
-    rings = [ring_y(i) for i in range(3)]
+    rings = [ring_y(i) for i in range(2)]
+    keep(gu_in.at[:, pl.ds(2 * (piece // 3), piece // 3), :], gu_late)
     for ring in rings:
         next(ring)
     for m in range(3):
@@ -827,7 +829,6 @@
         ].astype(F32)
     next(rings[0])
     next(rings[1])
-    next(rings[2])
     for copy in result.values():
         copy.wait_recv()
     result_ahead[0] = (block(down_v, 3, 0)[...].astype(F32) + res_up1[...].astype(F32)).astype(BF16)
@@ -859,6 +860,7 @@
     w_in,
     w_out,
     gu,
+    gl,
     dn,
     result_sum,
     ahead,
@@ -883,6 +885,7 @@
     w_in_v,
     w_out_v,
     gu_v,
+    gl_v,
     dn_v,
     down_v,
     gain_rows,
@@ -905,6 +908,11 @@
     result_rows,
     gu_n,
     gu_s,
+    gl_up1,
+    gl_down1,
+    gl_up2,
+    gl_down2,
+    gl_y,
     dn_up1,
     dn_down1,
     dn_up2,
@@ -998,8 +1006,8 @@
     own_rows, other_rows = even(col * rows, rows), even((1 - col) * rows, rows)
 
     def ffn_flow(i):
-        if i < 3:
-            height = gu.shape[0] // 3
+        if i < 2:
+            height = gu.shape[0] // 2
             start = i * height
             theirs, done = gu_n.at[i], gu_s.at[i]
             mine = gu_v.at[pl.ds(start, height), :]
@@ -1008,27 +1016,33 @@
             yield
             kept_wait(loads["gu"])
         else:
-            height = dn.shape[1]
-            start, mine, theirs, done = 0, dn_y, dn_n, dn_s
+            if i == 2:
+                held, loaded, name, height, start = gl, gl_v, "gl", gl.shape[1], 2 * gl.shape[1]
+                mine, theirs, done = gl_y, gu_n.at[2], gu_s.at[2]
+                one, two, three, four = gl_up1, gl_down1, gl_up2, gl_down2
+            else:
+                held, loaded, name, height, start = dn, dn_v, "dn", dn.shape[1], 0
+                mine, theirs, done = dn_y, dn_n, dn_s
+                one, two, three, four = dn_up1, dn_down1, dn_up2, dn_down2
             half = height // 2
-            low, high = pl.ds(start, half), pl.ds(start + half, half)
-            first = (mail.post(dn.at[2, low, :], dn_up1, right), mail.post(dn.at[2, high, :], dn_down1, left))
+            low, high = pl.ds(0, half), pl.ds(half, half)
+            first = (mail.post(held.at[2, low, :], one, right), mail.post(held.at[2, high, :], two, left))
             straight = (
-                mail.post(dn.at[1, high, :], dn_up2.at[pl.ds(half, half), :], right),
-                mail.post(dn.at[3, low, :], dn_down2.at[pl.ds(0, half), :], left),
+                mail.post(held.at[1, high, :], three.at[high, :], right),
+                mail.post(held.at[3, low, :], four.at[low, :], left),
             )
             yield
-            kept_wait(loads["dn"])
+            kept_wait(loads[name])
             first[0].wait_recv()
-            dn_up1[...] = plus(dn_v[1, low, :], dn_up1[...]).astype(BF16)
-            last = [mail.post(dn_up1, dn_up2.at[pl.ds(0, half), :], right)]
+            one[...] = plus(loaded[1, low, :], one[...]).astype(BF16)
+            last = [mail.post(one, three.at[low, :], right)]
             first[1].wait_recv()
-            dn_down1[...] = plus(dn_v[3, high, :], dn_down1[...]).astype(BF16)
-            last.append(mail.post(dn_down1, dn_down2.at[pl.ds(half, half), :], left))
+            two[...] = plus(loaded[3, high, :], two[...]).astype(BF16)
+            last.append(mail.post(two, four.at[high, :], left))
             yield
             for copy in straight + tuple(last):
                 copy.wait_recv()
-            mine[...] = plus(dn_v[0], dn_up2[...], dn_down2[...]).astype(BF16)
+            mine[...] = plus(loaded[0], three[...], four[...]).astype(BF16)
             swap = mail.post(mine, theirs, near)
             yield
         swap.wait_recv()
@@ -1160,11 +1174,13 @@
         ("normed", normed, normed_v),
         ("tok", tok, tok_v),
         ("dn", dn, dn_v),
+        ("gl", gl, gl_v),
         ("down", result_sum, down_v),
     ):
         loads[name] = keep(source, target)
     result_steps = result_flow()
-    next(flows[2])
+    next(flows[3])
+    next(flows[1])
     for j in range(4):
         gain_rows[:, j * piece : (j + 1) * piece] = gains[j]
 
@@ -1188,7 +1204,6 @@
     gains_own[...] = jnp.zeros_like(gains_own)
     for j in range(4):
         gains_own[j, 1:2, :] = 0.5 * gain_ffn_part[:, j * piece : (j + 1) * piece]
-    next(flows[3])
     next(result_steps)
     kept_wait(loads["w_out"])
     q_width = w_out.shape[0]
@@ -1201,6 +1216,8 @@
             lanes = slice(t * LANES, (t + 1) * LANES)
             target[lanes, 0 : source.shape[0]] = source[:, lanes].T
 
+    next(flows[0])
+    next(flows[3])
     kept_wait(loads["attended"])
     turn_over(attended_v, flat, q_width // LANES)
     for j in range(4):
@@ -1208,7 +1225,6 @@
             flat[0:q_width, :], grad_low[:, j * piece : (j + 1) * piece], preferred_element_type=F32
         ).astype(BF16)
     wo_steps = weight_flow(wo_p, wo_t, wo_up1, wo_down1, wo_up2, wo_down2, wo_s, wo_n, wo_z, wo_out)
-    next(flows[0])
 
     for name in ("query", "kva", "kvb", "ta", "tb"):
         kept_wait(loads[name])
@@ -1244,7 +1260,12 @@
     def low_sums(sums, part):
         return (sums[part, 0:HEAD_SIZE] * factor).astype(BF16), sums[part, HEAD_SIZE : 2 * HEAD_SIZE].astype(BF16)
 
+    next(wo_steps)
+    next(flows[1])
     next(flows[2])
+    next(result_steps)
+    next(flows[1])
+    next(flows[3])
     attend_back(1, kvb, turned_b_v, dkv_b)
     half_rows = kva.shape[0]
     low_part, high_part = slice(0, half_rows), slice(half_rows, 2 * half_rows)
@@ -1257,6 +1278,7 @@
         kv_got.append(mail.post(low_kv.at[part, :], from_near.at[step], near_of(place, other)))
         if step:
             kv_got.append(mail.post(own_kv.at[1, part, :], from_own.at[step - 1, 1], along_y(place, step)))
+    next(flows[0])
     attend_back(0, kva, turned_a_v, dkv_a)
     target = own_kv.at[0]
     target[:, 0:HEAD_SIZE], target[:, HEAD_SIZE : 2 * HEAD_SIZE] = low_sums(dkv_a, low_part)
@@ -1264,11 +1286,8 @@
         part = even(((row + step) % 4) * rows, rows)
         kv_got.append(mail.post(own_kv.at[0, part, :], from_own.at[step - 1, 0], along_y(place, step)))
     next(flows[2])
-    next(result_steps)
+    next(flows[3])
     next(wo_steps)
-    next(flows[3])
-    next(flows[1])
-    next(flows[0])
     kept_wait(loads["normed"])
     turn_over(normed_v, flat, width // LANES)
     for j in range(4):
@@ -1276,10 +1295,10 @@
             flat[j * piece : (j + 1) * piece, :], grad_pre[:, 0:q_width], preferred_element_type=F32
         ).astype(BF16)
     in_steps = weight_flow(in_p, in_t, in_up1, in_down1, in_up2, in_down2, in_s, in_n, in_z, in_out)
-    next(wo_steps)
     next(flows[3])
-    next(flows[1])
+    next(flows[2])
     next(flows[0])
+    next(in_steps)
     for copy in kv_got:
         copy.wait_recv()
     for half in range(2):
@@ -1294,8 +1313,8 @@
         grad_pre[part, q_width + HEAD_SIZE : q_width + 2 * HEAD_SIZE] = value[:, HEAD_SIZE : 2 * HEAD_SIZE].astype(
             BF16
         )
+    next(wo_steps)
     next(in_steps)
-    next(wo_steps)
     kept_wait(loads["w_in"])
     for j in range(4):
         grad_part[:, j * piece : (j + 1) * piece] = dot_nt(grad_pre[...], w_in_v[j]).astype(BF16)
@@ -1305,19 +1324,15 @@
             flat[j * piece : (j + 1) * piece, :], grad_pre[:, q_width:], preferred_element_type=F32
         ).astype(BF16)
     kw_steps = weight_flow(kw_p, kw_t, kw_up1, kw_down1, kw_up2, kw_down2, kw_s, kw_n, kw_z, kw_out)
+    next(wo_steps)
+    next(flows[2])
+    next(kw_steps)
+    next(result_steps)
     next(in_steps)
-    next(flows[3])
     next(kw_steps)
-    next(wo_steps)
     bias_own[...] = jnp.zeros_like(bias_own)
     bias_own[0:1, :] = jnp.sum(grad_pre[...].astype(F32), 0, keepdims=True)
-    next(in_steps)
     next(wo_steps)
-    next(in_steps)
-    next(flows[1])
-    next(kw_steps)
-    next(wo_steps)
-    next(kw_steps)
     kept_wait(loads["tok"])
     swap.wait_recv()
     back, gain_part = norm_back(
@@ -1326,9 +1341,10 @@
     rows_out[...] = (grad_middle[own_rows, :] + back).astype(BF16)
     for j in range(4):
         gains_own[j, 0:1, :] = gain_part[:, j * piece : (j + 1) * piece]
-    next(result_steps)
+    next(in_steps)
+    next(flows[2])
     next(kw_steps)
-    next(in_steps)
+    next(wo_steps)
     small_copies, small_kept = [], []
     for step in range(4):
         device = along_y(place, step)
@@ -1340,12 +1356,9 @@
             small_kept.append(keep(bias_own, bias_in.at[row]))
             small_kept.append(keep(gains_own.at[step], mine))
         small_copies.append(mail.post(gains_own.at[step], mine, pair_of(place, (row + step) % 4)))
-    next(wo_steps)
+    spread(rows_out, grad_out)
     next(kw_steps)
-    next(flows[3])
     next(in_steps)
-    spread(rows_out, grad_out)
-    next(result_steps)
     for copy in small_copies:
         copy.wait_recv()
     for index in small_kept:
@@ -1356,16 +1369,21 @@
         gains_in[0] + gains_in[1] + gains_in[2] + gains_in[3] + gains_in[4] + gains_in[5] + gains_in[6] + gains_in[7]
     )
     small_first = mail.post(small_a, small_t, twin)
+    next(result_steps)
+    next(kw_steps)
     small_first.wait_recv()
     small_b[...] = small_a[...] + small_t[...]
     small_second = mail.post(small_b, small_n, near)
     next(in_steps)
-    next(kw_steps)
+    next(flows[2])
     small_second.wait_recv()
     small_t[...] = small_b[...] + small_n[...]
     for device in (up, down, far_z):
         arrivals.append(mail.post(small_t, small_out.at[z], device))
     keep(small_t, small_out.at[z])
+    next(wo_steps)
+    next(kw_steps)
+    next(in_steps)
     for steps in [*flows, wo_steps, in_steps, kw_steps, result_steps]:
         for _ in steps:
             pass
@@ -1511,20 +1529,21 @@
 
     w_both_full = w_gu_full.reshape(width, 2 * share)
     half_block = (2, rows, width)
-    grad_normed_ffn, both_sum, down_half, result_sum, result_ahead = talk(
+    grad_normed_ffn, both_sum, both_late, down_half, result_sum, result_ahead = talk(
         ffn_kernel,
         4,
-        50,
-        14,
+        44,
+        15,
         [
             ((2 * rows, width), F32),
-            ((piece, share), BF16),
+            ((2 * piece // 3, share), BF16),
+            ((4, piece // 3, share), BF16),
             ((4, share // 2, piece), BF16),
             ((2 * rows, width), BF16),
             ((2, rows, width), BF16),
         ],
         [ANY] * 4,
-        [VMEM, VMEM, ANY, VMEM, VMEM],
+        [VMEM, VMEM, ANY, ANY, VMEM, VMEM],
         [
             pltpu.VMEM(shape, BF16)
             for shape in (
@@ -1551,10 +1570,10 @@
                 (rows, width),
                 (rows, width),
                 (rows, width),
-                (3, piece // 6, share),
-                (3, piece // 6, share),
-                (3, piece // 3, share),
-                (3, piece // 3, share),
+                (2, piece // 6, share),
+                (2, piece // 6, share),
+                (2, piece // 3, share),
+                (2, piece // 3, share),
             )
         ],
         limit=60,
@@ -1597,7 +1616,7 @@
             ((half_rows, piece), BF16),
             ((4, 16, in_width), F32),
         ],
-        [VMEM, ANY, ANY, VMEM] + [ANY] * 5 + [VMEM, ANY, VMEM] + [ANY] * 8,
+        [VMEM, ANY, ANY, VMEM] + [ANY] * 5 + [VMEM, ANY, VMEM] + [ANY] * 9,
         [ANY] * 8,
         scratch(F32, (2 * rows, width))
         + scratch(
@@ -1615,7 +1634,8 @@
             BF16,
             (4, piece, in_width),
             (q_width, width),
-            (piece, share),
+            (2 * thirds, share),
+            (4, thirds, share),
             (4, share // 2, piece),
             (2 * rows, width),
         )
@@ -1636,6 +1656,11 @@
             (rows, width),
             gu_chunk,
             gu_chunk,
+            halved((thirds, share)),
+            halved((thirds, share)),
+            (thirds, share),
+            (thirds, share),
+            (thirds, share),
             halved(dn_chunk),
             halved(dn_chunk),
             dn_chunk,
@@ -1670,6 +1695,7 @@
         w_in_full,
         w_out_full,
         both_sum,
+        both_late,
         down_half,
         result_sum,
         result_ahead,

time: 283 us -> 279 us (0.986)
  Pallas kernels: 278 us -> 274 us
    pallas_call x1, Pallas kernels: 83.2 us -> 79.8 us  [on_device(): talk(ffn_kernel, 4, 44, 15, [((2 * rows, width), F32), ((2 * piece // 3,...]
where the time goes in v2:
time: 279 us; the launch traced here: 274 us
  Pallas kernels  274 us (98%)
    pallas_call x1, Pallas kernels, on_device(): talk(front_kernel, 0, FRONT_COPIES, FRONT_LOCAL, [((2 * rows, width), BF1...  89.9 us
    pallas_call x1, Pallas kernels, on_device(): talk(back_kernel, 8, BACK_COPIES, BACK_LOCAL, [((2, piece, 4 * share), BF...  89.8 us
    pallas_call x1, Pallas kernels, on_device(): talk(ffn_kernel, 4, 44, 15, [((2 * rows, width), F32), ((2 * piece // 3,...  79.8 us
    pallas_call x1, Pallas kernels, on_device(): pl.pallas_call(widen_kernel, grid=(steps,), out_shape=[jax.ShapeDtypeStru...  14.1 us

profile of v2, /device:TPU:1, one launch (start us, length us, event | category | flops | bytes accessed | tf_op | source)
XLA Modules:
  0.0 274.5 jit_solution(15740426544516546049)
XLA Ops:
  0.7 89.9 %shard_map.254 = (bf16[256,1536]{1,0:T(8,128)(2,1)}, bf16[4,256,1536]{2,1,0:T(8,128)(2,1)}, f32[4,8,384]{2,1,0:T(8,128)}, bf16[256,1536]{1,0:T(8,128)(2,1)}, bf1...) custom-call(bf16[512,384]{1,0:T(8,128)(2,1)} %tok.1, ...), custom_call_target="tpu_custom_call" | custom-call | tf_op jit(solution)/shard_map/pallas_call | solution.py:1464
  90.5 79.8 %shard_map.255 = (f32[256,1536]{1,0:T(8,128)}, bf16[256,1152]{1,0:T(8,128)(2,1)}, bf16[4,128,1152]{2,1,0:T(8,128)(2,1)}, bf16[4,576,384]{2,1,0:T(8,128)(2,1)}, b...) custom-call(bf16[256,1536]{1,0:T(8,128)(2,1)} %get-tuple-element.60.normed, ...), custom_call_target="tpu_custom_call" | custom-call | tf_op jit(solution)/shard_map/pallas_call | solution.py:1532
  170.3 89.8 %shard_map.256 = (bf16[2,384,4608]{2,1,0:T(8,128)(2,1)}, bf16[4608,384]{1,0:T(8,128)(2,1)}, bf16[384,768]{1,0:T(8,128)(2,1)}, bf16[384,256]{1,0:T(8,128)(2,1)}, ...) custom-call(f32[256,1536]{1,0:T(8,128)} %get-tuple-element.64.total, ...), custom_call_target="tpu_custom_call" | custom-call | tf_op jit(solution)/shard_map/pallas_call | solution.py:1604
  260.2 14.1 %shard_map.257 = (f32[512,384]{1,0:T(8,128)}, f32[512,384]{1,0:T(8,128)}, f32[384,768]{1,0:T(8,128)}, f32[384,128]{1,0:T(8,128)}, f32[384,128]{1,0:T(8,128)}, /*...) custom-call(bf16[2,384,4608]{2,1,0:T(8,128)(2,1)} %get-tuple-element, ...), custom_call_target="tpu_custom_call" | custom-call | tf_op jit(solution)/shard_map/pallas_call | solution.py:1727

commit v3 on v2

--- a/solution.py
+++ b/solution.py
@@ -468,6 +468,10 @@
     a_got, b_got = [], []
     for step in (1, 2, 3):
         a_got.append(mail.post(kv.at[a_rows, :], kva.at[spot, :], along_y(place, step)))
+    for step in range(4):
+        b_got.append(mail.post(kv.at[a_rows, :], kvb.at[spot, :], near_of(place, (row + step) % 4)))
+        if step:
+            b_got.append(mail.post(kv.at[b_rows, :], kvb.at[high_spot, :], along_y(place, step)))
     kva[spot, :] = kv[a_rows, :]
     kvb[high_spot, :] = kv[b_rows, :]
     for first in range(0, q_width, 2 * HEAD_SIZE):
@@ -515,53 +519,50 @@
         for j, block in enumerate(normalise(value, 1)):
             normed_ffn[part, j * piece : (j + 1) * piece] = block
 
-    def z_send(source, target, half):
-        part = pl.ds(half * rows, rows)
-        return (
-            mail.post(source.at[part, :], target.at[1, part, :], up),
-            mail.post(source.at[part, :], target.at[3, part, :], down),
-        )
-
-    def z_forward(target, half, copies):
-        part = pl.ds(half * rows, rows)
-        if half == 0:
-            copies[0].wait_recv()
-            return copies[1], mail.post(target.at[1, part, :], target.at[2, part, :], up)
-        copies[1].wait_recv()
-        return copies[0], mail.post(target.at[3, part, :], target.at[2, part, :], down)
-
+    def z_part(slot, half):
+        return cot_full.at[slot, pl.ds(half * rows, rows), :]
+
+    def z_send():
+        copies = {}
+        for turn in range(2):
+            copies["u", turn] = mail.post(z_part(0, turn), z_part(1, turn), up)
+            copies["d", 1 - turn] = mail.post(z_part(0, 1 - turn), z_part(3, 1 - turn), down)
+        return copies
+
+    def z_forward(copies):
+        copies["u", 0].wait_recv()
+        far_up = mail.post(z_part(1, 0), z_part(2, 0), up)
+        copies["d", 1].wait_recv()
+        far_down = mail.post(z_part(3, 1), z_part(2, 1), down)
+        return [copies["u", 1], copies["d", 0], far_up, far_down]
+
+    cot_pair.wait_recv()
+    cot_z = z_send()
     for copy in a_got:
         copy.wait_recv()
-    for step in range(4):
-        b_got.append(mail.post(kv.at[a_rows, :], kvb.at[spot, :], near_of(place, (row + step) % 4)))
-        if step:
-            b_got.append(mail.post(kv.at[b_rows, :], kvb.at[high_spot, :], along_y(place, step)))
     keep(kva, kva_out)
     z_third(out_parts, out_far)
     for copy in shares:
         copy.wait_recv()
     keep(w_out, w_out_out)
     swap_a = attend(0, kva, bias_a)
-    cot_pair.wait_recv()
-    cot_z = [z_send(cot_full.at[0], cot_full, half) for half in range(2)]
     for copy in b_got:
         copy.wait_recv()
     keep(kvb, kvb_out)
+    y_start("wd", wd_source, wd_part)
     swap_b = attend(1, kvb, bias_b)
     y_end("gu", gu_part, near_gu, near)
-    y_start("wd", wd_source, wd_part)
     finish_half(0, swap_a)
-    cot_last = [z_forward(cot_full, half, cot_z[half]) for half in range(2)]
     y_forward("wd", wd_part)
+    cot_last = z_forward(cot_z)
+    y_share("wd", wd_part, twins, twin)
     finish_half(1, swap_b)
-    y_share("wd", wd_part, twins, twin)
     for j, copy in zip((3, 1, 2), near_gu):
         copy.wait_recv()
         twins.append(mail.post(gu_whole(j), gu_whole(j), twin))
     y_end("wd", wd_part, twins, twin)
-    for copies in cot_last:
-        for copy in copies:
-            copy.wait_recv()
+    for copy in cot_last:
+        copy.wait_recv()
     for copy in twins:
         copy.wait_recv()
     for copy in kept:

time: 279 us -> 268 us (0.961)
  Pallas kernels: 274 us -> 263 us
    pallas_call x1, Pallas kernels: 89.9 us -> 81.7 us  [on_device(): talk(front_kernel, 0, FRONT_COPIES, FRONT_LOCAL, [((2 * rows, width), BF1...]
where the time goes in v3:
time: 268 us; the launch traced here: 264 us
  Pallas kernels  263 us (98%)
    pallas_call x1, Pallas kernels, on_device(): talk(back_kernel, 8, BACK_COPIES, BACK_LOCAL, [((2, piece, 4 * share), BF...  87.2 us
    pallas_call x1, Pallas kernels, on_device(): talk(front_kernel, 0, FRONT_COPIES, FRONT_LOCAL, [((2 * rows, width), BF1...  81.7 us
    pallas_call x1, Pallas kernels, on_device(): talk(ffn_kernel, 4, 44, 15, [((2 * rows, width), F32), ((2 * piece // 3,...  79.7 us
    pallas_call x1, Pallas kernels, on_device(): pl.pallas_call(widen_kernel, grid=(steps,), out_shape=[jax.ShapeDtypeStru...  14.1 us

profile of v3, /device:TPU:1, one launch (start us, length us, event | category | flops | bytes accessed | tf_op | source)
XLA Modules:
  0.0 263.7 jit_solution(9753771249583374039)
XLA Ops:
  0.7 81.7 %shard_map.254 = (bf16[256,1536]{1,0:T(8,128)(2,1)}, bf16[4,256,1536]{2,1,0:T(8,128)(2,1)}, f32[4,8,384]{2,1,0:T(8,128)}, bf16[256,1536]{1,0:T(8,128)(2,1)}, bf1...) custom-call(bf16[512,384]{1,0:T(8,128)(2,1)} %tok.1, ...), custom_call_target="tpu_custom_call" | custom-call | tf_op jit(solution)/shard_map/pallas_call | solution.py:1465
  82.4 79.7 %shard_map.255 = (f32[256,1536]{1,0:T(8,128)}, bf16[256,1152]{1,0:T(8,128)(2,1)}, bf16[4,128,1152]{2,1,0:T(8,128)(2,1)}, bf16[4,576,384]{2,1,0:T(8,128)(2,1)}, b...) custom-call(bf16[256,1536]{1,0:T(8,128)(2,1)} %get-tuple-element.60.normed, ...), custom_call_target="tpu_custom_call" | custom-call | tf_op jit(solution)/shard_map/pallas_call | solution.py:1533
  162.1 87.2 %shard_map.256 = (bf16[2,384,4608]{2,1,0:T(8,128)(2,1)}, bf16[4608,384]{1,0:T(8,128)(2,1)}, bf16[384,768]{1,0:T(8,128)(2,1)}, bf16[384,256]{1,0:T(8,128)(2,1)}, ...) custom-call(f32[256,1536]{1,0:T(8,128)} %get-tuple-element.64.total, ...), custom_call_target="tpu_custom_call" | custom-call | tf_op jit(solution)/shard_map/pallas_call | solution.py:1605
  249.4 14.1 %shard_map.257 = (f32[512,384]{1,0:T(8,128)}, f32[512,384]{1,0:T(8,128)}, f32[384,768]{1,0:T(8,128)}, f32[384,128]{1,0:T(8,128)}, f32[384,128]{1,0:T(8,128)}, /*...) custom-call(bf16[2,384,4608]{2,1,0:T(8,128)(2,1)} %get-tuple-element, ...), custom_call_target="tpu_custom_call" | custom-call | tf_op jit(solution)/shard_map/pallas_call | solution.py:1728

commit v4 on v3

--- a/solution.py
+++ b/solution.py
@@ -21,7 +21,7 @@
 FRONT_COPIES = 77
 FRONT_LOCAL = 27
 BACK_COPIES = 145
-BACK_LOCAL = 28
+BACK_LOCAL = 30
 
 
 def here():
@@ -126,12 +126,12 @@
     tok_out,
     cot_full,
     gains_out,
-    normed,
+    normed_t,
     query,
     kva_out,
     kvb_out,
     logs,
-    attended,
+    attended_t,
     tables,
     middle,
     turned_a,
@@ -141,6 +141,10 @@
     w_out_out,
     wgu_full,
     wd_full,
+    keys_a_t,
+    keys_b_t,
+    normed,
+    attended,
     lens,
     gains,
     tok_v,
@@ -511,6 +515,10 @@
             ).astype(BF16)
         return mail.post(branch.at[part, :], branch_in.at[part, :], pair)
 
+    def turn_over(source, target):
+        for first in range(0, source.shape[1], LANES):
+            target[first : first + LANES, :] = source[:, first : first + LANES].T
+
     def finish_half(half, copy):
         part = slice(half * rows, (half + 1) * rows)
         copy.wait_recv()
@@ -538,6 +546,7 @@
 
     cot_pair.wait_recv()
     cot_z = z_send()
+    turn_over(normed, normed_t)
     for copy in a_got:
         copy.wait_recv()
     keep(kva, kva_out)
@@ -552,6 +561,10 @@
     y_start("wd", wd_source, wd_part)
     swap_b = attend(1, kvb, bias_b)
     y_end("gu", gu_part, near_gu, near)
+    turn_over(attended, attended_t)
+    for keys, target in ((kva, keys_a_t), (kvb, keys_b_t)):
+        for first in range(0, keys.shape[0], LANES):
+            target[:, first : first + LANES] = keys[first : first + LANES, 0:HEAD_SIZE].T
     finish_half(0, swap_a)
     y_forward("wd", wd_part)
     cot_last = z_forward(cot_z)
@@ -853,6 +866,8 @@
     query,
     kv_a,
     kv_b,
+    keys_a_t,
+    keys_b_t,
     logs,
     attended,
     tables,
@@ -880,6 +895,8 @@
     query_v,
     kva,
     kvb,
+    kta,
+    ktb,
     attended_v,
     turned_a_v,
     turned_b_v,
@@ -893,8 +910,6 @@
     grad_middle,
     grad_low,
     grad_att,
-    flat,
-    keys_t,
     dkv_a,
     dkv_b,
     low_kv,
@@ -1168,6 +1183,8 @@
         ("query", query, query_v),
         ("kva", kv_a, kva),
         ("kvb", kv_b, kvb),
+        ("kta", keys_a_t, kta),
+        ("ktb", keys_b_t, ktb),
         ("ta", turned_a, turned_a_v),
         ("tb", turned_b, turned_b_v),
         ("gu", gu, gu_v),
@@ -1212,22 +1229,14 @@
         lanes = slice(first, first + 256)
         grad_att[:, lanes] = dot_nt(grad_low[...], w_out_v[lanes, :]).astype(BF16)
 
-    def turn_over(source, target, count):
-        for t in range(count):
-            lanes = slice(t * LANES, (t + 1) * LANES)
-            target[lanes, 0 : source.shape[0]] = source[:, lanes].T
-
-    next(flows[0])
-    next(flows[3])
     kept_wait(loads["attended"])
-    turn_over(attended_v, flat, q_width // LANES)
     for j in range(4):
         wo_p[j] = jnp.dot(
-            flat[0:q_width, :], grad_low[:, j * piece : (j + 1) * piece], preferred_element_type=F32
+            attended_v[...], grad_low[:, j * piece : (j + 1) * piece], preferred_element_type=F32
         ).astype(BF16)
     wo_steps = weight_flow(wo_p, wo_t, wo_up1, wo_down1, wo_up2, wo_down2, wo_s, wo_n, wo_z, wo_out)
 
-    for name in ("query", "kva", "kvb", "ta", "tb"):
+    for name in ("query", "kva", "kvb", "kta", "ktb", "ta", "tb"):
         kept_wait(loads[name])
     heads = q_width // HEAD_SIZE
     factor = HEAD_SIZE ** (-0.5)
@@ -1236,12 +1245,8 @@
         part = slice(half * rows, (half + 1) * rows)
         return value * tables[0, part, :] + pltpu.roll(value * tables[1, part, :], HEAD_SIZE // 2, 1)
 
-    def attend_back(half, keys, mask, sums):
+    def attend_back(half, keys, keys_t, mask, sums):
         part = slice(half * rows, (half + 1) * rows)
-        count = keys.shape[0]
-        for t in range(count // LANES):
-            lanes = slice(t * LANES, (t + 1) * LANES)
-            keys_t[:, lanes] = keys[lanes, 0:HEAD_SIZE].T
         sums[...] = jnp.zeros_like(sums)
 
         @pl.loop(0, heads)
@@ -1255,7 +1260,7 @@
             grad_scores = (probs * (grad_probs - inner)).astype(BF16)
             sums[:, 0:HEAD_SIZE] += jnp.dot(grad_scores, one, preferred_element_type=F32)
             sums[:, HEAD_SIZE : 2 * HEAD_SIZE] += jnp.dot(probs.astype(BF16), grad, preferred_element_type=F32)
-            grad_query = jnp.dot(keys_t[:, 0:count], grad_scores, preferred_element_type=F32).T * factor
+            grad_query = jnp.dot(keys_t[...], grad_scores, preferred_element_type=F32).T * factor
             grad_pre[part, lanes] = unrotate(grad_query, half).astype(BF16)
 
     def low_sums(sums, part):
@@ -1267,7 +1272,7 @@
     next(result_steps)
     next(flows[1])
     next(flows[3])
-    attend_back(1, kvb, turned_b_v, dkv_b)
+    attend_back(1, kvb, ktb, turned_b_v, dkv_b)
     half_rows = kva.shape[0]
     low_part, high_part = slice(0, half_rows), slice(half_rows, 2 * half_rows)
     for target, sums, part in ((low_kv, dkv_b, low_part), (own_kv.at[1], dkv_b, high_part)):
@@ -1280,7 +1285,7 @@
         if step:
             kv_got.append(mail.post(own_kv.at[1, part, :], from_own.at[step - 1, 1], along_y(place, step)))
     next(flows[0])
-    attend_back(0, kva, turned_a_v, dkv_a)
+    attend_back(0, kva, kta, turned_a_v, dkv_a)
     target = own_kv.at[0]
     target[:, 0:HEAD_SIZE], target[:, HEAD_SIZE : 2 * HEAD_SIZE] = low_sums(dkv_a, low_part)
     for step in (1, 2, 3):
@@ -1290,10 +1295,9 @@
     next(flows[3])
     next(wo_steps)
     kept_wait(loads["normed"])
-    turn_over(normed_v, flat, width // LANES)
     for j in range(4):
         in_p[j] = jnp.dot(
-            flat[j * piece : (j + 1) * piece, :], grad_pre[:, 0:q_width], preferred_element_type=F32
+            normed_v[j * piece : (j + 1) * piece, :], grad_pre[:, 0:q_width], preferred_element_type=F32
         ).astype(BF16)
     in_steps = weight_flow(in_p, in_t, in_up1, in_down1, in_up2, in_down2, in_s, in_n, in_z, in_out)
     next(flows[3])
@@ -1322,7 +1326,7 @@
     swap = mail.post(grad_part.at[other_rows, :], grad_in, pair)
     for j in range(4):
         kw_p[j] = jnp.dot(
-            flat[j * piece : (j + 1) * piece, :], grad_pre[:, q_width:], preferred_element_type=F32
+            normed_v[j * piece : (j + 1) * piece, :], grad_pre[:, q_width:], preferred_element_type=F32
         ).astype(BF16)
     kw_steps = weight_flow(kw_p, kw_t, kw_up1, kw_down1, kw_up2, kw_down2, kw_s, kw_n, kw_z, kw_out)
     next(wo_steps)
@@ -1447,12 +1451,12 @@
         tok_rows,
         cot_full,
         gains4,
-        normed,
+        normed_t,
         query,
         kv_a,
         kv_b,
         logs,
-        attended,
+        attended_t,
         tables,
         middle,
         mask_a,
@@ -1462,6 +1466,8 @@
         w_out_full,
         w_gu_full,
         w_down_full,
+        keys_a_t,
+        keys_b_t,
     ) = talk(
         front_kernel,
         0,
@@ -1471,12 +1477,12 @@
             ((2 * rows, width), BF16),
             ((4, 2 * rows, width), BF16),
             ((4, 8, piece), F32),
-            ((2 * rows, width), BF16),
+            ((width, 2 * rows), BF16),
             ((2 * rows, q_width), BF16),
             ((half_rows, 2 * kv_width), BF16),
             ((2 * half_rows, 2 * kv_width), BF16),
             ((2 * heads, 8, rows), F32),
-            ((2 * rows, q_width), BF16),
+            ((q_width, 2 * rows), BF16),
             ((2, 2 * rows, HEAD_SIZE), F32),
             ((2 * rows, width), F32),
             ((half_rows, rows), F32),
@@ -1486,10 +1492,14 @@
             ((q_width, width), BF16),
             ((4, 2, thin, 2 * share), BF16),
             ((share, width), BF16),
+            ((HEAD_SIZE, half_rows), BF16),
+            ((HEAD_SIZE, 2 * half_rows), BF16),
         ],
         [ANY] * 2 + [VMEM] * 6 + [ANY] * 7,
-        [ANY] * 3 + [VMEM] * 2 + [ANY] * 2 + [VMEM] * 7 + [ANY] * 4,
+        [ANY] * 3 + [VMEM] * 2 + [ANY] * 2 + [VMEM] * 7 + [ANY] * 4 + [VMEM] * 2,
         [
+            pltpu.VMEM((2 * rows, width), BF16),
+            pltpu.VMEM((2 * rows, q_width), BF16),
             pltpu.VMEM((8, LANES), jnp.int32),
             pltpu.VMEM((8, piece), F32),
             pltpu.VMEM((2 * rows, width), BF16),
@@ -1617,18 +1627,20 @@
             ((half_rows, piece), BF16),
             ((4, 16, in_width), F32),
         ],
-        [VMEM, ANY, ANY, VMEM] + [ANY] * 5 + [VMEM, ANY, VMEM] + [ANY] * 9,
+        [VMEM, ANY, ANY, VMEM] + [ANY] * 7 + [VMEM, ANY, VMEM] + [ANY] * 9,
         [ANY] * 8,
         scratch(F32, (2 * rows, width))
         + scratch(
             BF16,
             (2 * rows, width),
             (2 * rows, width),
-            (2 * rows, width),
+            (width, 2 * rows),
             (2 * rows, q_width),
             (half_rows, 2 * kv_width),
             (2 * half_rows, 2 * kv_width),
-            (2 * rows, q_width),
+            (HEAD_SIZE, half_rows),
+            (HEAD_SIZE, 2 * half_rows),
+            (q_width, 2 * rows),
         )
         + scratch(F32, (half_rows, rows), (2 * half_rows, rows))
         + scratch(
@@ -1641,7 +1653,7 @@
             (2 * rows, width),
         )
         + scratch(F32, (8, width), (2 * rows, width))
-        + scratch(BF16, (2 * rows, width), (2 * rows, q_width), (width, 2 * rows), (HEAD_SIZE, 2 * half_rows))
+        + scratch(BF16, (2 * rows, width), (2 * rows, q_width))
         + scratch(F32, (half_rows, 2 * kv_width), (2 * half_rows, 2 * kv_width))
         + scratch(
             BF16,
@@ -1684,12 +1696,14 @@
         cot_full,
         gains4,
         tok_rows,
-        normed,
+        normed_t,
         query,
         kv_a,
         kv_b,
+        keys_a_t,
+        keys_b_t,
         logs,
-        attended,
+        attended_t,
         tables,
         mask_a,
         mask_b,

time: 268 us -> 291 us (1.086)
  Pallas kernels: 263 us -> 285 us
    pallas_call x1, Pallas kernels: 87.2 us -> 110 us  [on_device(): talk(back_kernel, 8, BACK_COPIES, BACK_LOCAL, [((2, piece, 4 * share), BF...]
where the time goes in v4:
time: 291 us; the launch traced here: 286 us
  Pallas kernels  285 us (98%)
    pallas_call x1, Pallas kernels, on_device(): talk(back_kernel, 8, BACK_COPIES, BACK_LOCAL, [((2, piece, 4 * share), BF...  110 us
    pallas_call x1, Pallas kernels, on_device(): talk(front_kernel, 0, FRONT_COPIES, FRONT_LOCAL, [((2 * rows, width), BF1...  81.8 us
    pallas_call x1, Pallas kernels, on_device(): talk(ffn_kernel, 4, 44, 15, [((2 * rows, width), F32), ((2 * piece // 3,...  79.7 us
    pallas_call x1, Pallas kernels, on_device(): pl.pallas_call(widen_kernel, grid=(steps,), out_shape=[jax.ShapeDtypeStru...  14.1 us

profile of v4, /device:TPU:1, one launch (start us, length us, event | category | flops | bytes accessed | tf_op | source)
XLA Modules:
  0.0 286.3 jit_solution(5232996317859603603)
XLA Ops:
  0.7 81.8 %shard_map.254 = (bf16[256,1536]{1,0:T(8,128)(2,1)}, bf16[4,256,1536]{2,1,0:T(8,128)(2,1)}, f32[4,8,384]{2,1,0:T(8,128)}, bf16[1536,256]{1,0:T(8,128)(2,1)}, bf1...) custom-call(bf16[512,384]{1,0:T(8,128)(2,1)} %tok.1, ...), custom_call_target="tpu_custom_call" | custom-call | tf_op jit(solution)/shard_map/pallas_call | solution.py:1471
  82.5 79.7 %shard_map.255 = (f32[256,1536]{1,0:T(8,128)}, bf16[256,1152]{1,0:T(8,128)(2,1)}, bf16[4,128,1152]{2,1,0:T(8,128)(2,1)}, bf16[4,576,384]{2,1,0:T(8,128)(2,1)}, b...) custom-call(bf16[256,1536]{1,0:T(8,128)(2,1)} %get-tuple-element.62.normed, ...), custom_call_target="tpu_custom_call" | custom-call | tf_op jit(solution)/shard_map/pallas_call | solution.py:1543
  162.3 109.7 %shard_map.256 = (bf16[2,384,4608]{2,1,0:T(8,128)(2,1)}, bf16[4608,384]{1,0:T(8,128)(2,1)}, bf16[384,768]{1,0:T(8,128)(2,1)}, bf16[384,256]{1,0:T(8,128)(2,1)}, ...) custom-call(f32[256,1536]{1,0:T(8,128)} %get-tuple-element.66.total, ...), custom_call_target="tpu_custom_call" | custom-call | tf_op jit(solution)/shard_map/pallas_call | solution.py:1615
  272.0 14.1 %shard_map.257 = (f32[512,384]{1,0:T(8,128)}, f32[512,384]{1,0:T(8,128)}, f32[384,768]{1,0:T(8,128)}, f32[384,128]{1,0:T(8,128)}, f32[384,128]{1,0:T(8,128)}, /*...) custom-call(bf16[2,384,4608]{2,1,0:T(8,128)(2,1)} %get-tuple-element, ...), custom_call_target="tpu_custom_call" | custom-call | tf_op jit(solution)/shard_map/pallas_call | solution.py:1742

commit v5 on v3

--- a/solution.py
+++ b/solution.py
@@ -712,10 +712,10 @@
     def forward(i):
         rows_i = pl.ds(i * size, size)
         first["u", i].wait_recv()
-        stage_up[i] = (block(parts, 3, 0).at[rows_i, :][...].astype(F32) + up1[i].astype(F32)).astype(BF16)
+        stage_up[i] = (block(parts, 3, 0).at[rows_i, :][...] + up1[i])
         second["u", 0, i] = mail.post(stage_up.at[i], up2.at[0, rows_i, :], up)
         first["d", i].wait_recv()
-        stage_down[i] = (block(parts, 1, 1).at[rows_i, :][...].astype(F32) + down1[i].astype(F32)).astype(BF16)
+        stage_down[i] = (block(parts, 1, 1).at[rows_i, :][...] + down1[i])
         second["d", 1, i] = mail.post(stage_down.at[i], down2.at[1, rows_i, :], down)
 
     turn_over(x, turned)
@@ -754,7 +754,7 @@
     gu_tiles(tiles // 2 + 1, tiles)
     for j in range(4):
         shared[j].wait_recv()
-        gu_in[j] = (wgu_v[pl.ds(j * piece, piece), mine].astype(F32) + gu_in[j].astype(F32)).astype(BF16)
+        gu_in[j] = (wgu_v[pl.ds(j * piece, piece), mine] + gu_in[j])
 
     def ring_y(i):
         height = piece // 3
@@ -768,10 +768,10 @@
         ]
         yield
         begin[0].wait_recv()
-        one[...] = (gu_in[1, low, :].astype(F32) + one[...].astype(F32)).astype(BF16)
+        one[...] = (gu_in[1, low, :] + one[...])
         straight.append(mail.post(one, three.at[pl.ds(0, half), :], right))
         begin[1].wait_recv()
-        two[...] = (gu_in[3, high, :].astype(F32) + two[...].astype(F32)).astype(BF16)
+        two[...] = (gu_in[3, high, :] + two[...])
         straight.append(mail.post(two, four.at[pl.ds(half, half), :], left))
         yield
         for copy in straight:
@@ -820,7 +820,7 @@
         next(ring)
     for j in range(4):
         shared[4 + j].wait_recv()
-        dn_in[j] = (wd_v[rows_mine, pl.ds(j * piece, piece)].astype(F32) + dn_in[j].astype(F32)).astype(BF16)
+        dn_in[j] = (wd_v[rows_mine, pl.ds(j * piece, piece)] + dn_in[j])
         keep(dn_in.at[j], dn_half.at[j])
     for half, i in ((0, 0), (1, 0), (0, 1), (1, 1)):
         rows_i = pl.ds(i * size, size)
@@ -832,8 +832,8 @@
     next(rings[1])
     for copy in result.values():
         copy.wait_recv()
-    result_ahead[0] = (block(down_v, 3, 0)[...].astype(F32) + res_up1[...].astype(F32)).astype(BF16)
-    result_ahead[1] = (block(down_v, 1, 1)[...].astype(F32) + res_down1[...].astype(F32)).astype(BF16)
+    result_ahead[0] = (block(down_v, 3, 0)[...] + res_up1[...])
+    result_ahead[1] = (block(down_v, 1, 1)[...] + res_down1[...])
     for half, theirs in ((0, res_down2), (1, res_up2)):
         value = block(down_v, 0, half)[...].astype(F32) + theirs[...].astype(F32)
         result_sum[pl.ds(half * rows, rows), :] = value.astype(BF16)
@@ -1035,10 +1035,10 @@
             yield
             kept_wait(loads[name])
             first[0].wait_recv()
-            one[...] = plus(loaded[1, low, :], one[...]).astype(BF16)
+            one[...] = (loaded[1, low, :] + one[...])
             last = [mail.post(one, three.at[low, :], right)]
             first[1].wait_recv()
-            two[...] = plus(loaded[3, high, :], two[...]).astype(BF16)
+            two[...] = (loaded[3, high, :] + two[...])
             last.append(mail.post(two, four.at[high, :], left))
             yield
             for copy in straight + tuple(last):
@@ -1047,7 +1047,7 @@
             swap = mail.post(mine, theirs, near)
             yield
         swap.wait_recv()
-        done[...] = plus(mine[...], theirs[...]).astype(BF16)
+        done[...] = (mine[...] + theirs[...])
 
         def room(slot, which=None):
             begin, size = (start, height) if which is None else (start + which * half, half)
@@ -1091,7 +1091,7 @@
         yield
         copy.wait_recv()
         for j in range(4):
-            t[j] = plus(part[j, even(core * height, height), :], t[j]).astype(BF16)
+            t[j] = (part[j, even(core * height, height), :] + t[j])
         first = (mail.post(t.at[2, low, :], up1, right), mail.post(t.at[2, high, :], down1, left))
         straight = (
             mail.post(t.at[1, high, :], up2.at[high, :], right),
@@ -1099,10 +1099,10 @@
         )
         yield
         first[0].wait_recv()
-        up1[...] = plus(t[1, low, :], up1[...]).astype(BF16)
+        up1[...] = (t[1, low, :] + up1[...])
         last = [mail.post(up1, up2.at[low, :], right)]
         first[1].wait_recv()
-        down1[...] = plus(t[3, high, :], down1[...]).astype(BF16)
+        down1[...] = (t[3, high, :] + down1[...])
         last.append(mail.post(down1, down2.at[high, :], left))
         yield
         for copy in straight + tuple(last):
@@ -1111,7 +1111,7 @@
         swap = mail.post(total_h, theirs, near)
         yield
         swap.wait_recv()
-        t[0] = plus(total_h[...], theirs[...]).astype(BF16)
+        t[0] = (total_h[...] + theirs[...])
         size = height // 4
         copies = []
         for step, device in ((1, up), (3, down), (2, far_z)):
@@ -1141,7 +1141,7 @@
         for half, copy in enumerate(copies):
             copy.wait_recv()
             part = pl.ds(half * rows, rows)
-            res_total[part, :] = plus(down_v[part, :], res_in[half]).astype(BF16)
+            res_total[part, :] = (down_v[part, :] + res_in[half])
         swap = mail.post(res_total.at[other_rows, :], part_in, pair)
         yield
         swap.wait_recv()

time: 268 us -> 269 us (level)
  no operation moved by 1% of the time
where the time goes in v5:
time: 269 us; the launch traced here: 265 us
  Pallas kernels  264 us (98%)
    pallas_call x1, Pallas kernels, on_device(): talk(back_kernel, 8, BACK_COPIES, BACK_LOCAL, [((2, piece, 4 * share), BF...  88.3 us
    pallas_call x1, Pallas kernels, on_device(): talk(front_kernel, 0, FRONT_COPIES, FRONT_LOCAL, [((2 * rows, width), BF1...  81.7 us
    pallas_call x1, Pallas kernels, on_device(): talk(ffn_kernel, 4, 44, 15, [((2 * rows, width), F32), ((2 * piece // 3,...  79.4 us
    pallas_call x1, Pallas kernels, on_device(): pl.pallas_call(widen_kernel, grid=(steps,), out_shape=[jax.ShapeDtypeStru...  14.1 us

profile of v5, /device:TPU:1, one launch (start us, length us, event | category | flops | bytes accessed | tf_op | source)
XLA Modules:
  0.0 264.8 jit_solution(12246830989989271378)
XLA Ops:
  0.7 81.7 %shard_map.254 = (bf16[256,1536]{1,0:T(8,128)(2,1)}, bf16[4,256,1536]{2,1,0:T(8,128)(2,1)}, f32[4,8,384]{2,1,0:T(8,128)}, bf16[256,1536]{1,0:T(8,128)(2,1)}, bf1...) custom-call(bf16[512,384]{1,0:T(8,128)(2,1)} %tok.1, ...), custom_call_target="tpu_custom_call" | custom-call | tf_op jit(solution)/shard_map/pallas_call | solution.py:1465
  82.4 79.4 %shard_map.255 = (f32[256,1536]{1,0:T(8,128)}, bf16[256,1152]{1,0:T(8,128)(2,1)}, bf16[4,128,1152]{2,1,0:T(8,128)(2,1)}, bf16[4,576,384]{2,1,0:T(8,128)(2,1)}, b...) custom-call(bf16[256,1536]{1,0:T(8,128)(2,1)} %get-tuple-element.60.normed, ...), custom_call_target="tpu_custom_call" | custom-call | tf_op jit(solution)/shard_map/pallas_call | solution.py:1533
  161.8 88.3 %shard_map.256 = (bf16[2,384,4608]{2,1,0:T(8,128)(2,1)}, bf16[4608,384]{1,0:T(8,128)(2,1)}, bf16[384,768]{1,0:T(8,128)(2,1)}, bf16[384,256]{1,0:T(8,128)(2,1)}, ...) custom-call(f32[256,1536]{1,0:T(8,128)} %get-tuple-element.64.total, ...), custom_call_target="tpu_custom_call" | custom-call | tf_op jit(solution)/shard_map/pallas_call | solution.py:1605
  250.2 14.1 %shard_map.257 = (f32[512,384]{1,0:T(8,128)}, f32[512,384]{1,0:T(8,128)}, f32[384,768]{1,0:T(8,128)}, f32[384,128]{1,0:T(8,128)}, f32[384,128]{1,0:T(8,128)}, /*...) custom-call(bf16[2,384,4608]{2,1,0:T(8,128)(2,1)} %get-tuple-element, ...), custom_call_target="tpu_custom_call" | custom-call | tf_op jit(solution)/shard_map/pallas_call | solution.py:1728
